TPU v7x, 32 devices: a whole 2x2x4 slice. The times are simulated.
32 devices in a mesh: seq: 16 (over z, y, x), head: 2 (over core).
Axes of the slice: x: 2, y: 2, z: 4, core: 2. Of those that a mesh axis runs over, the one named last changes fastest.
Arguments:
- layer_input: bfloat16 [4, 2, 1024, 768], P(None, None, 'seq'), may hold values from -6 to 6
- block_sizes: int32 [4], replicated, may hold values from 4 to 16, as said below
- mixing_gain: float32 [768], replicated, may hold values from 0.5 to 1.5
- mixing_shift: float32 [768], replicated, may hold values from -2 to 2
- w_heads: bfloat16 [3, 768, 768], P(None, None, 'head'), may hold values from -0.21875 to 0.21875
- w_output: bfloat16 [768, 768], P('head'), may hold values from -6 to 6
- feed_gain: float32 [768], replicated, may hold values from 0.5 to 1.5
- feed_shift: float32 [768], replicated, may hold values from -2 to 2
- w_up: bfloat16 [768, 3072], P(None, 'head'), may hold values from -0.21875 to 0.21875
- bias_up: float32 [3072], P('head'), may hold values from -3 to 3
- w_down: bfloat16 [3072, 768], P('head'), may hold values from -0.109375 to 0.109375
- bias_down: float32 [768], replicated, may hold values from -2 to 2
- cotangent: bfloat16 [4, 2, 1024, 768], P(None, None, 'seq'), may hold values from -6 to 6
Outputs:
- layer_output: bfloat16 [4, 2, 1024, 768], P(None, None, 'seq')
- input_grad: float32 [4, 2, 1024, 768], P(None, None, 'seq')
- grad_heads: float32 [3, 768, 768], P(None, None, 'head')
- grad_output: float32 [768, 768], P('head')
- grad_up: float32 [768, 3072], P(None, 'head')
- grad_bias_up: float32 [3072], P('head')
- grad_down: float32 [3072, 768], P('head')
- grad_bias_down: float32 [768], replicated
- grad_mixing_gain: float32 [768], replicated
- grad_mixing_shift: float32 [768], replicated
- grad_feed_gain: float32 [768], replicated
- grad_feed_shift: float32 [768], replicated
Inputs may be any that keep to these rules, and one draw needn't show every extreme that they name: `block_sizes`: each example's block size is 4, 8 or 16, and every draw holds all three.
All inputs are finite; a program needn't handle non-finite values.
Results may differ from a plain program's by a relative error of at most 0.02.
Values may be sent and summed in bfloat16 or wider, within the bound.
A program may use at most 256 MiB of HBM per device.

v0:
```python
import math

import jax
import jax.numpy as jnp
from jax import lax
from jax.sharding import PartitionSpec as P

HD = 64


neg_large = -1e30
norm_eps = 1e-05
rotary_base = 10000.0


def layer_norm(inputs, norm_gain, norm_shift):
    center = jnp.mean(inputs, axis=-1, keepdims=True)
    offsets = inputs - center
    spread = jnp.mean(offsets * offsets, axis=-1, keepdims=True)
    return offsets * lax.rsqrt(spread + norm_eps) * norm_gain + norm_shift


def gelu_tanh(pre_values):
    return jax.nn.gelu(pre_values, approximate=True)


def rotary_tables(positions, head_size):
    halves = head_size // 2
    frequency = jnp.exp(jnp.arange(halves, dtype=jnp.float32) * (-math.log(rotary_base) / halves))
    angles = positions.astype(jnp.float32)[:, None] * frequency[None, :]
    return (jnp.cos(angles), jnp.sin(angles))


def rotate(vectors, cos_table, sin_table):
    halves = vectors.shape[-1] // 2
    front_half = vectors[..., :halves]
    back_half = vectors[..., halves:]
    cos_wide = cos_table[:, None, :]
    sin_wide = sin_table[:, None, :]
    return jnp.concatenate(
        [
            front_half * cos_wide - back_half * sin_wide,
            back_half * cos_wide + front_half * sin_wide,
        ],
        axis=-1,
    )


def rotate_back(gradient, cos_table, sin_table):
    halves = gradient.shape[-1] // 2
    front_half = gradient[..., :halves]
    back_half = gradient[..., halves:]
    cos_wide = cos_table[:, None, :]
    sin_wide = sin_table[:, None, :]
    return jnp.concatenate(
        [
            front_half * cos_wide + back_half * sin_wide,
            back_half * cos_wide - front_half * sin_wide,
        ],
        axis=-1,
    )


def clean_allowed(query_blocks, query_clean, key_blocks):
    earlier = key_blocks[None, :] < query_blocks[:, None]
    within = key_blocks[None, :] == query_blocks[:, None]
    return earlier | query_clean[:, None] & within


def noisy_allowed(query_blocks, query_clean, key_blocks):
    return jnp.logical_not(query_clean)[:, None] & (key_blocks[None, :] == query_blocks[:, None])


def block_rows(row_total):
    return row_total if row_total <= 1024 else math.gcd(row_total, 1024)


def attend_block(running, queries, key_part, value_part, allowed, score_scale):
    row_max, totals, summed = running
    scores = (
        jnp.einsum("qhd,khd->hqk", queries, key_part, preferred_element_type=jnp.float32)
        * score_scale
    )
    masked = jnp.where(allowed[None], scores, neg_large)
    new_max = jnp.maximum(row_max, jnp.max(masked, axis=-1))
    weights = jnp.where(allowed[None], jnp.exp(masked - new_max[..., None]), 0.0)
    rescale = jnp.exp(row_max - new_max)
    totals = totals * rescale + jnp.sum(weights, axis=-1)
    summed = summed * rescale[..., None] + jnp.einsum(
        "hqk,khd->hqd", weights.astype(jnp.bfloat16), value_part, preferred_element_type=jnp.float32
    )
    return (new_max, totals, summed)


def block_gradients(
    query_part, grad_part, log_part, delta_part, key_part, value_part, allowed, score_scale
):
    scores = (
        jnp.einsum("qhd,khd->hqk", query_part, key_part, preferred_element_type=jnp.float32)
        * score_scale
    )
    masked = jnp.where(allowed[None], scores, neg_large)
    softmaxed = jnp.where(allowed[None], jnp.exp(masked - log_part[..., None]), 0.0)
    grad_values = jnp.einsum(
        "hqk,qhd->khd",
        softmaxed.astype(jnp.bfloat16),
        grad_part,
        preferred_element_type=jnp.float32,
    )
    grad_probs = jnp.einsum(
        "qhd,khd->hqk", grad_part, value_part, preferred_element_type=jnp.float32
    )
    grad_scores = (softmaxed * (grad_probs - delta_part[..., None])).astype(jnp.bfloat16)
    grad_queries = (
        jnp.einsum("hqk,khd->qhd", grad_scores, key_part, preferred_element_type=jnp.float32)
        * score_scale
    )
    grad_keys = (
        jnp.einsum("hqk,qhd->khd", grad_scores, query_part, preferred_element_type=jnp.float32)
        * score_scale
    )
    return (grad_queries, grad_keys, grad_values)


def local(
    layer_input,
    block_sizes,
    mixing_gain,
    mixing_shift,
    w_heads,
    w_output,
    feed_gain,
    feed_shift,
    w_up,
    bias_up,
    w_down,
    bias_down,
    cotangent,
):
    micro_count = layer_input.shape[0]
    local_len = layer_input.shape[2]
    model_width = layer_input.shape[3]
    head_width = w_heads.shape[2]
    head_count = head_width // HD
    total_len = local_len * lax.axis_size("seq")
    score_scale = 1.0 / math.sqrt(HD)
    own_rank = lax.axis_index("seq")
    own_last = (own_rank + 1) * local_len - 1
    own_positions = own_rank * local_len + jnp.arange(local_len, dtype=jnp.int32)
    row_positions = jnp.concatenate([own_positions, own_positions])
    row_clean = jnp.arange(2 * local_len, dtype=jnp.int32) >= local_len
    cos_table, sin_table = rotary_tables(row_positions, HD)
    grad_heads = jnp.zeros(w_heads.shape, jnp.float32)
    grad_output = jnp.zeros(w_output.shape, jnp.float32)
    grad_up = jnp.zeros(w_up.shape, jnp.float32)
    grad_bias_up = jnp.zeros(bias_up.shape, jnp.float32)
    grad_down = jnp.zeros(w_down.shape, jnp.float32)
    grad_bias_down = jnp.zeros(bias_down.shape, jnp.float32)
    grad_mixing_gain = jnp.zeros(mixing_gain.shape, jnp.float32)
    grad_mixing_shift = jnp.zeros(mixing_shift.shape, jnp.float32)
    grad_feed_gain = jnp.zeros(feed_gain.shape, jnp.float32)
    grad_feed_shift = jnp.zeros(feed_shift.shape, jnp.float32)
    outputs = []
    input_grads = []
    for micro_index in range(micro_count):
        block_len = block_sizes[micro_index]
        row_blocks = row_positions // block_len
        inputs = layer_input[micro_index].reshape(2 * local_len, model_width).astype(jnp.float32)
        normed_one = layer_norm(inputs, mixing_gain, mixing_shift).astype(jnp.bfloat16)
        projected = jnp.einsum(
            "rd,kdc->krc", normed_one, w_heads, preferred_element_type=jnp.float32
        )
        shaped = projected.reshape(3, 2 * local_len, head_count, HD)
        queries = rotate(shaped[0], cos_table, sin_table).astype(jnp.bfloat16)
        keys_rot = rotate(shaped[1], cos_table, sin_table).astype(jnp.bfloat16)
        values_all = shaped[2].astype(jnp.bfloat16)
        noisy_ok = noisy_allowed(row_blocks, row_clean, row_blocks[:local_len])
        start_state = (
            jnp.full((head_count, 2 * local_len), neg_large, jnp.float32),
            jnp.zeros((head_count, 2 * local_len), jnp.float32),
            jnp.zeros((head_count, 2 * local_len, HD), jnp.float32),
        )
        running = attend_block(
            start_state,
            queries,
            keys_rot[:local_len],
            values_all[:local_len],
            noisy_ok,
            score_scale,
        )
        clean_keys = keys_rot[local_len:].reshape(local_len, head_width)
        clean_values = values_all[local_len:].reshape(local_len, head_width)
        carried = running
        key_part = lax.all_gather(clean_keys, "seq", axis=0, tiled=True)
        row_total = key_part.shape[0]
        block_size = block_rows(row_total)
        block_count = row_total // block_size

        def one_block(inner, block_inputs):
            offset, key_block, value_block = block_inputs
            key_first = offset

            def one_compute(state):
                key_blocks = (key_first + jnp.arange(block_size, dtype=jnp.int32)) // block_len
                allowed = clean_allowed(row_blocks, row_clean, key_blocks)
                return attend_block(
                    state,
                    queries,
                    key_block.reshape(block_size, head_count, HD),
                    value_block.reshape(block_size, head_count, HD),
                    allowed,
                    score_scale,
                )

            return (lax.cond(key_first > own_last, lambda state: state, one_compute, inner), None)

        carried, unused = lax.scan(
            one_block,
            carried,
            (
                jnp.arange(block_count, dtype=jnp.int32) * block_size,
                key_part.reshape(block_count, block_size, head_width),
                lax.all_gather(clean_values, "seq", axis=0, tiled=True).reshape(
                    block_count, block_size, head_width
                ),
            ),
        )
        running = carried
        row_max, totals, summed = running
        attended = summed / totals[..., None]
        log_totals = row_max + jnp.log(totals)
        attended_rows = (
            attended.transpose(1, 0, 2).reshape(2 * local_len, head_width).astype(jnp.bfloat16)
        )
        mixed = lax.psum(
            jnp.dot(attended_rows, w_output, preferred_element_type=jnp.float32).astype(
                jnp.bfloat16
            ),
            "head",
        ).astype(jnp.float32)
        middle = inputs + mixed
        normed_two = layer_norm(middle, feed_gain, feed_shift).astype(jnp.bfloat16)
        hidden_pre = jnp.dot(normed_two, w_up, preferred_element_type=jnp.float32) + bias_up
        hidden = gelu_tanh(hidden_pre).astype(jnp.bfloat16)
        fed = lax.psum(
            jnp.dot(hidden, w_down, preferred_element_type=jnp.float32).astype(jnp.bfloat16), "head"
        ).astype(jnp.float32)
        result = middle + fed + bias_down
        outputs.append(result.astype(jnp.bfloat16).reshape(2, local_len, model_width))
        upstream = cotangent[micro_index].reshape(2 * local_len, model_width)
        upstream_f = upstream.astype(jnp.float32)
        grad_bias_down = grad_bias_down + jnp.sum(upstream_f, axis=0)
        grad_down = grad_down + jnp.einsum(
            "rf,rd->fd", hidden, upstream, preferred_element_type=jnp.float32
        )
        grad_hidden = jnp.einsum("rd,fd->rf", upstream, w_down, preferred_element_type=jnp.float32)
        unused_gelu, pull_gelu = jax.vjp(gelu_tanh, hidden_pre)
        grad_pre = pull_gelu(grad_hidden)[0].astype(jnp.bfloat16)
        grad_bias_up = grad_bias_up + jnp.sum(grad_pre.astype(jnp.float32), axis=0)
        grad_up = grad_up + jnp.einsum(
            "rd,rf->df", normed_two, grad_pre, preferred_element_type=jnp.float32
        )
        back_two = lax.psum(
            jnp.einsum("rf,df->rd", grad_pre, w_up, preferred_element_type=jnp.float32).astype(
                jnp.bfloat16
            ),
            "head",
        ).astype(jnp.float32)
        unused_two, pull_two = jax.vjp(layer_norm, middle, feed_gain, feed_shift)
        middle_part, gain_part, shift_part = pull_two(back_two)
        grad_feed_gain = grad_feed_gain + gain_part
        grad_feed_shift = grad_feed_shift + shift_part
        grad_middle = upstream_f + middle_part
        grad_mixed = grad_middle.astype(jnp.bfloat16)
        grad_output = grad_output + jnp.einsum(
            "rc,rd->cd", attended_rows, grad_mixed, preferred_element_type=jnp.float32
        )
        grad_attended = (
            jnp.einsum("rd,cd->rc", grad_mixed, w_output, preferred_element_type=jnp.float32)
            .astype(jnp.bfloat16)
            .reshape(2 * local_len, head_count, HD)
        )
        row_delta = jnp.sum(
            grad_attended.astype(jnp.float32) * attended.transpose(1, 0, 2), axis=-1
        ).T
        local_queries, noisy_keys, noisy_values = block_gradients(
            queries,
            grad_attended,
            log_totals,
            row_delta,
            keys_rot[:local_len],
            values_all[:local_len],
            noisy_ok,
            score_scale,
        )
        back_keys, back_values = (
            lax.all_gather(clean_keys, "seq", axis=0, tiled=True),
            lax.all_gather(clean_values, "seq", axis=0, tiled=True),
        )
        key_size = block_rows(total_len)
        key_count = total_len // key_size

        def query_side(carried, block_inputs):
            offset, key_block, value_block = block_inputs

            def query_compute(state):
                key_blocks = (offset + jnp.arange(key_size, dtype=jnp.int32)) // block_len
                allowed = clean_allowed(row_blocks, row_clean, key_blocks)
                grads_part = block_gradients(
                    queries,
                    grad_attended,
                    log_totals,
                    row_delta,
                    key_block.reshape(key_size, head_count, HD),
                    value_block.reshape(key_size, head_count, HD),
                    allowed,
                    score_scale,
                )
                return state + grads_part[0]

            return (lax.cond(offset > own_last, lambda state: state, query_compute, carried), None)

        grad_queries, unused = lax.scan(
            query_side,
            local_queries,
            (
                jnp.arange(key_count, dtype=jnp.int32) * key_size,
                back_keys.reshape(key_count, key_size, head_width),
                back_values.reshape(key_count, key_size, head_width),
            ),
        )
        all_queries, all_grads = (
            lax.all_gather(queries.reshape(2 * local_len, head_width), "seq", axis=0, tiled=True),
            lax.all_gather(
                grad_attended.reshape(2 * local_len, head_width), "seq", axis=0, tiled=True
            ),
        )
        all_logs, all_deltas = (
            lax.all_gather(log_totals.T, "seq", axis=0, tiled=True),
            lax.all_gather(row_delta.T, "seq", axis=0, tiled=True),
        )
        query_total = all_queries.shape[0]
        query_size = block_rows(query_total)
        query_count = query_total // query_size
        own_key_blocks = own_positions // block_len
        own_keys = keys_rot[local_len:]
        own_values = values_all[local_len:]

        def key_side(carried, block_inputs):
            offset, query_block, grad_block, log_block, delta_block = block_inputs
            last_owner = (offset + query_size - 1) // (2 * local_len)

            def key_compute(state):
                row_index = offset + jnp.arange(query_size, dtype=jnp.int32)
                owner_rank = row_index // (2 * local_len)
                within = row_index % (2 * local_len)
                query_blocks = (owner_rank * local_len + within % local_len) // block_len
                allowed = clean_allowed(query_blocks, within >= local_len, own_key_blocks)
                grads_part = block_gradients(
                    query_block.reshape(query_size, head_count, HD),
                    grad_block.reshape(query_size, head_count, HD),
                    log_block.T,
                    delta_block.T,
                    own_keys,
                    own_values,
                    allowed,
                    score_scale,
                )
                return (state[0] + grads_part[1], state[1] + grads_part[2])

            return (
                lax.cond(last_owner < own_rank, lambda state: state, key_compute, carried),
                None,
            )

        zero_grads = jnp.zeros((local_len, head_count, HD), jnp.float32)
        own_grads, unused = lax.scan(
            key_side,
            (zero_grads, zero_grads),
            (
                jnp.arange(query_count, dtype=jnp.int32) * query_size,
                all_queries.reshape(query_count, query_size, head_width),
                all_grads.reshape(query_count, query_size, head_width),
                all_logs.reshape(query_count, query_size, head_count),
                all_deltas.reshape(query_count, query_size, head_count),
            ),
        )
        clean_key_grads, clean_value_grads = own_grads
        grad_keys_all = jnp.concatenate([noisy_keys, clean_key_grads], axis=0)
        grad_values_all = jnp.concatenate([noisy_values, clean_value_grads], axis=0)
        grad_query_pre = rotate_back(grad_queries, cos_table, sin_table).astype(jnp.bfloat16)
        grad_key_pre = rotate_back(grad_keys_all, cos_table, sin_table).astype(jnp.bfloat16)
        grad_values_low = grad_values_all.astype(jnp.bfloat16)
        grad_projected = jnp.stack([grad_query_pre, grad_key_pre, grad_values_low]).reshape(
            3, 2 * local_len, head_width
        )
        grad_heads = grad_heads + jnp.einsum(
            "rd,krc->kdc", normed_one, grad_projected, preferred_element_type=jnp.float32
        )
        back_one = lax.psum(
            jnp.einsum(
                "krc,kdc->rd", grad_projected, w_heads, preferred_element_type=jnp.float32
            ).astype(jnp.bfloat16),
            "head",
        ).astype(jnp.float32)
        unused_one, pull_one = jax.vjp(layer_norm, inputs, mixing_gain, mixing_shift)
        input_part, gain_one, shift_one = pull_one(back_one)
        grad_mixing_gain = grad_mixing_gain + gain_one
        grad_mixing_shift = grad_mixing_shift + shift_one
        input_grads.append((grad_middle + input_part).reshape(2, local_len, model_width))
    summed_grads = lax.psum(
        (
            grad_heads,
            grad_output,
            grad_up,
            grad_bias_up,
            grad_down,
            grad_bias_down,
            grad_mixing_gain,
            grad_mixing_shift,
            grad_feed_gain,
            grad_feed_shift,
        ),
        "seq",
    )
    return (
        jnp.stack(outputs),
        jnp.stack(input_grads),
        summed_grads[0],
        summed_grads[1],
        summed_grads[2],
        summed_grads[3],
        summed_grads[4],
        summed_grads[5],
        summed_grads[6],
        summed_grads[7],
        summed_grads[8],
        summed_grads[9],
    )


def solution(mesh):
    in_specs = (
        P(None, None, "seq", None),
        P(),
        P(),
        P(),
        P(None, None, "head"),
        P("head", None),
        P(),
        P(),
        P(None, "head"),
        P("head"),
        P("head", None),
        P(),
        P(None, None, "seq", None),
    )
    out_specs = (
        P(None, None, "seq", None),
        P(None, None, "seq", None),
        P(None, None, "head"),
        P("head", None),
        P(None, "head"),
        P("head"),
        P("head", None),
        P(),
        P(),
        P(),
        P(),
        P(),
    )
    return jax.shard_map(local, mesh=mesh, in_specs=in_specs, out_specs=out_specs, check_vma=False)
```

profile of v0, /device:TPU:0, one launch (start us, length us, event | category | flops | bytes accessed | tf_op | source)
XLA Modules:
  0.0 1755.2 jit_solution(3074743448630543462)
XLA Ops:
  62.0 3.3 and_select_fusion.2
  69.4 49.4 %all_gather.84 = bf16[1024,384]{1,0:T(8,128)(2,1)} all-gather(bf16[64,384]{1,0:T(8,128)(2,1)S(1)} %reshape.2466), channel_id=1, replica_groups=mesh['seq'=16,'head'=2] {'seq'}, dimensions={0}, use_global_device_ids=true | all-gather | bytes 835584 | tf_op jit(solution)/shard_map/all_gather | solution.py:194
  118.8 3.2 multiply_subtract_fusion.2
  125.8 42.3 %all-gather.2 = bf16[1,1024,384]{2,1,0:T(8,128)(2,1)} all-gather(bf16[1,64,384]{2,1,0:T(8,128)(2,1)S(1)} %get-tuple-element.3627), channel_id=4, replica_groups=mesh['seq'=16,'head'=2] {'seq'}, dimensions={1}, use_global_device_ids=true | all-gather | bytes 835584 | tf_op jit(solution)/shard_map/all_gather | solution.py:223
  168.4 14.6 conditional.14
  189.6 44.9 %all_gather.86 = bf16[1024,384]{1,0:T(8,128)(2,1)} all-gather(bf16[64,384]{1,0:T(8,128)(2,1)S(1)} %reshape.2468), channel_id=1, replica_groups=mesh['seq'=16,'head'=2] {'seq'}, dimensions={0}, use_global_device_ids=true | all-gather | bytes 835584 | tf_op jit(solution)/shard_map/all_gather | solution.py:194
  241.9 42.6 %all-gather.3 = bf16[1,1024,384]{2,1,0:T(8,128)(2,1)} all-gather(bf16[1,64,384]{2,1,0:T(8,128)(2,1)} %get-tuple-element.3629), channel_id=5, replica_groups=mesh['seq'=16,'head'=2] {'seq'}, dimensions={1}, use_global_device_ids=true | all-gather | bytes 835584 | tf_op jit(solution)/shard_map/all_gather | solution.py:223
  286.3 17.2 conditional.15
  308.7 44.9 %all_gather.80 = bf16[1024,384]{1,0:T(8,128)(2,1)} all-gather(bf16[64,384]{1,0:T(8,128)(2,1)S(1)} %reshape.2462), channel_id=1, replica_groups=mesh['seq'=16,'head'=2] {'seq'}, dimensions={0}, use_global_device_ids=true | all-gather | bytes 835584 | tf_op jit(solution)/shard_map/all_gather | solution.py:194
  360.4 44.1 %all-gather = bf16[1,1024,384]{2,1,0:T(8,128)(2,1)} all-gather(bf16[1,64,384]{2,1,0:T(8,128)(2,1)} %get-tuple-element.3625), channel_id=2, replica_groups=mesh['seq'=16,'head'=2] {'seq'}, dimensions={1}, use_global_device_ids=true | all-gather | bytes 835584 | tf_op jit(solution)/shard_map/all_gather | solution.py:223
  406.4 17.1 conditional.12
  419.7 3.9 fusion.90
  426.9 43.2 %all_gather.82 = bf16[1024,384]{1,0:T(8,128)(2,1)} all-gather(bf16[64,384]{1,0:T(8,128)(2,1)S(1)} %reshape.2464), channel_id=1, replica_groups=mesh['seq'=16,'head'=2] {'seq'}, dimensions={0}, use_global_device_ids=true | all-gather | bytes 835584 | tf_op jit(solution)/shard_map/all_gather | solution.py:194
  473.9 43.8 %all-gather.1 = bf16[1,1024,384]{2,1,0:T(8,128)(2,1)} all-gather(bf16[1,64,384]{2,1,0:T(8,128)(2,1)S(1)} %get-tuple-element.3623), channel_id=3, replica_groups=mesh['seq'=16,'head'=2] {'seq'}, dimensions={1}, use_global_device_ids=true | all-gather | bytes 835584 | tf_op jit(solution)/shard_map/all_gather | solution.py:223
  517.6 3.4 fusion.476
  522.0 17.4 conditional.13
  535.5 3.8 fusion.105
  547.4 3.5 convert_reduce_fusion.1
  559.4 39.1 %all_gather.97 = f32[2048,6]{0,1:T(8,128)} all-gather(f32[128,6]{0,1:T(8,128)S(1)} %bitcast.791), channel_id=1, replica_groups=mesh['seq'=16,'head'=2] {'seq'}, dimensions={0}, use_global_device_ids=true | all-gather | bytes 52224 | tf_op jit(solution)/shard_map/all_gather | solution.py:339
  599.1 39.6 %all_gather.101 = f32[2048,6]{0,1:T(8,128)} all-gather(f32[128,6]{0,1:T(8,128)S(1)} %bitcast.790), channel_id=1, replica_groups=mesh['seq'=16,'head'=2] {'seq'}, dimensions={0}, use_global_device_ids=true | all-gather | bytes 52224 | tf_op jit(solution)/shard_map/all_gather | solution.py:339
  641.3 3.6 fusion.477
  655.3 39.4 %all_gather.93 = f32[2048,6]{0,1:T(8,128)} all-gather(f32[128,6]{0,1:T(8,128)} %bitcast.788), channel_id=1, replica_groups=mesh['seq'=16,'head'=2] {'seq'}, dimensions={0}, use_global_device_ids=true | all-gather | bytes 52224 | tf_op jit(solution)/shard_map/all_gather | solution.py:339
  701.0 39.9 %all_gather.89 = f32[2048,6]{0,1:T(8,128)} all-gather(f32[128,6]{0,1:T(8,128)} %bitcast.789), channel_id=1, replica_groups=mesh['seq'=16,'head'=2] {'seq'}, dimensions={0}, use_global_device_ids=true | all-gather | bytes 52224 | tf_op jit(solution)/shard_map/all_gather | solution.py:339
  741.5 3.2 convolution_convert_fusion.6
  757.2 12.4 conditional.18
  758.4 3.5 fusion.472
  765.2 4.0 fusion.167
  769.6 39.9 %all_gather.99 = f32[2048,6]{0,1:T(8,128)} all-gather(f32[128,6]{0,1:T(8,128)} %fusion.331), channel_id=1, replica_groups=mesh['seq'=16,'head'=2] {'seq'}, dimensions={0}, use_global_device_ids=true | all-gather | bytes 52224 | tf_op jit(solution)/shard_map/all_gather | solution.py:340
  835.7 11.0 all-gather.23.cloned.1.call-done
  849.3 35.7 %while.134 = (s32[]{:T(128)}, f32[64,6,64]{2,0,1:T(8,128)S(1)}, f32[64,6,64]{2,0,1:T(8,128)S(1)}, s32[2]{0:T(128)}, s32[]{:T(128)}, /*index=5*/s32[]{:T(128)}, b...) while((s32[]{:T(128)}, f32[64,6,64]{2,0,1:T(8,128)S(1)}, ...), condition=%wide.region_83.84_spmd.clone.clone, body=%wide.region_80.83_spmd.clone.clone.sunk | while | flops 204864080 | bytes 12186793 | solution.py:377
  853.7 13.5 conditional.34
  871.5 13.5 conditional.34
  892.9 3.5 fusion.332
  896.5 11.6 all-reduce.14.cloned.1.call-done
  927.2 4.2 fusion.425
  937.5 14.2 all-reduce.20.cloned.1.call-done
  962.1 8.9 add_add_fusion.1
  971.2 3.2 add_add_fusion
  1005.3 12.3 conditional.17
  1006.5 3.4 fusion.471
  1013.5 3.8 fusion.157
  1019.2 17.8 %conditional.16 = (f32[128,6,32]{2,0,1:T(8,128)}, f32[128,6,32]{2,0,1:T(8,128)}) conditional(s32[]{:T(128)} %convert_element_type.639, (s32[]{:T(128)}, s32[128]{0:T(128)}, pred[128]{0:T(512)(128)(4,1)}, bf16[1024,384]{1,0:T(8,128)(2,1)}, bf16[128,6,64]{2,0,1:T(8,128)(2,1)S(1)}, /*index=5*/f32[6,128]{1,0:T(8,128)}, ...), branch_computations={%region_52.53_spmd.clone, %region_53.54_spmd.clone} | conditional | flops 308125696 | bytes 13477136 | solution.py:321
  1021.6 3.4 fusion.470
  1029.5 4.7 fusion.147
  1037.1 12.3 conditional.19
  1038.2 3.4 fusion.473
  1045.1 3.9 fusion.177
  1053.2 44.2 %all_gather.103 = f32[2048,6]{0,1:T(8,128)} all-gather(f32[128,6]{0,1:T(8,128)} %copy-done.194), channel_id=1, replica_groups=mesh['seq'=16,'head'=2] {'seq'}, dimensions={0}, use_global_device_ids=true | all-gather | bytes 52224 | tf_op jit(solution)/shard_map/all_gather | solution.py:340
  1097.4 38.8 %all_gather.95 = f32[2048,6]{0,1:T(8,128)} all-gather(f32[128,6]{0,1:T(8,128)} %copy-done.195), channel_id=1, replica_groups=mesh['seq'=16,'head'=2] {'seq'}, dimensions={0}, use_global_device_ids=true | all-gather | bytes 52224 | tf_op jit(solution)/shard_map/all_gather | solution.py:340
  1136.2 40.2 %all_gather.91 = f32[2048,6]{0,1:T(8,128)} all-gather(f32[128,6]{0,1:T(8,128)} %copy-done.196), channel_id=1, replica_groups=mesh['seq'=16,'head'=2] {'seq'}, dimensions={0}, use_global_device_ids=true | all-gather | bytes 52224 | tf_op jit(solution)/shard_map/all_gather | solution.py:340
  1188.2 28.1 %while.135 = (s32[]{:T(128)}, f32[64,6,64]{2,0,1:T(8,128)S(1)}, f32[64,6,64]{2,0,1:T(8,128)S(1)}, s32[2]{0:T(128)}, s32[]{:T(128)}, /*index=5*/s32[]{:T(128)}, b...) while((s32[]{:T(128)}, f32[64,6,64]{2,0,1:T(8,128)S(1)}, ...), condition=%wide.region_96.97_spmd.clone.clone, body=%wide.region_93.96_spmd.clone.clone.sunk | while | flops 204864080 | bytes 11793521 | solution.py:377
  1191.5 10.7 conditional.35
  1205.6 10.7 conditional.35
  1220.4 31.6 %while.133 = (s32[]{:T(128)}, f32[64,6,64]{2,0,1:T(8,128)S(1)}, f32[64,6,64]{2,0,1:T(8,128)}, s32[2]{0:T(128)}, s32[]{:T(128)}, /*index=5*/s32[]{:T(128)}, bf16[...) while((s32[]{:T(128)}, f32[64,6,64]{2,0,1:T(8,128)S(1)}, ...), condition=%wide.region_70.71_spmd.clone.clone, body=%wide.region_67.70_spmd.clone.clone.sunk | while | flops 204864080 | bytes 11793521 | solution.py:377
  1223.9 12.4 conditional.33
  1239.7 12.4 conditional.33
  1258.1 27.9 %while.132 = (s32[]{:T(128)}, f32[64,6,64]{2,0,1:T(8,128)S(1)}, f32[64,6,64]{2,0,1:T(8,128)S(1)}, s32[2]{0:T(128)}, s32[]{:T(128)}, /*index=5*/s32[]{:T(128)}, b...) while((s32[]{:T(128)}, f32[64,6,64]{2,0,1:T(8,128)S(1)}, ...), condition=%wide.region_57.58_spmd.clone.clone, body=%wide.region_54.57_spmd.clone.clone.sunk | while | flops 204864080 | bytes 11793521 | solution.py:377
  1261.5 10.7 conditional.32
  1275.4 10.7 conditional.32
  1318.2 7.4 all-reduce.18.cloned.1.call-done
  1330.6 81.0 %all-reduce = (f32[1536]{0:T(1024)}, f32[768]{0:T(1024)}, f32[768]{0:T(1024)}, f32[768]{0:T(1024)}, f32[768]{0:T(1024)}, /*index=5*/f32[768]{0:T(1024)}) all-reduce(f32[1536]{0:T(1024)S(1)} %add_add_fusion.18, f32[768]{0:T(1024)S(1)} %add_add_fusion.23, f32[768]{0:T(1024)S(1)} %add_add_fusion.22, ...), channel_id=1, replica_groups=mesh['seq'=16,'head'=2] {'seq'}, use_global_device_ids=true, to_apply=%region_107.108 | all-reduce | flops 5376 | bytes 43008 | tf_op jit(solution)/shard_map/psum | solution.py:411
  1418.0 315.3 %all-reduce.16.cloned.1.call-done = (f32[3,768,384]{1,2,0:T(8,128)}, f32[384,768]{1,0:T(8,128)}, f32[768,1536]{1,0:T(8,128)}, f32[1536,768]{1,0:T(8,128)}) async-done(((f32[3,768,384]{1,2,0:T(8,128)}, f32[384,768]{1,0:T(8,128)}, f32[768,1536]{1,0:T(8,128)}, f32[1536,768]{1,0:T(8,128)}), (f32[3,768,384]{1,2,0:T(8,128)}, f32[384,768]{1,0:T(8,128)}, f32[768,1536]{1,0:T(8,128)}, ...) | async-done | bytes 14155792 | tf_op jit(solution)/shard_map/psum | solution.py:411
  1733.3 5.2 copy.242
  1739.6 5.5 copy.476
  (1069 shorter events, 511.3 us)
Async XLA Ops:
  8.0 539.3 %copy-start = (bf16[768,1536]{1,0:T(8,128)(2,1)S(1)}, bf16[768,1536]{1,0:T(8,128)(2,1)}, u32[]{:S(2)}) copy-start(bf16[768,1536]{1,0:T(8,128)(2,1)} %param.53) | copy-start | bytes 7077892
  8.0 535.0 %all-reduce.12.cloned.1.call-start = ((), (), s32[]{:S(2)}) async-start(), calls=%async_computation | async-start | bytes 393216 | tf_op jit(solution)/shard_map/psum | solution.py:235
  65.7 53.2 %copy-start.67 = (f32[128,32]{1,0:T(8,128)}, f32[128,32]{1,0:T(8,128)S(1)}, u32[]{:S(2)}) copy-start(f32[128,32]{1,0:T(8,128)S(1)} %get-tuple-element.3677) | copy-start | bytes 49156
  65.7 53.1 %copy-start.68 = (f32[128,32]{1,0:T(8,128)}, f32[128,32]{1,0:T(8,128)S(1)}, u32[]{:S(2)}) copy-start(f32[128,32]{1,0:T(8,128)S(1)} %get-tuple-element.3678) | copy-start | bytes 49156
  68.8 54.8 %copy-start.113 = (bf16[64,6,64]{2,0,1:T(8,128)(2,1)}, bf16[64,6,64]{2,0,1:T(8,128)(2,1)S(1)}, u32[]{:S(2)}) copy-start(bf16[64,6,64]{2,0,1:T(8,128)(2,1)S(1)} %get-tuple-element.3619) | copy-start | bytes 147460
  69.4 53.4 %copy-start.198 = (s32[128]{0:T(128)S(1)}, s32[128]{0:T(128)}, u32[]{:S(2)}) copy-start(s32[128]{0:T(128)} %get-tuple-element.3684) | copy-start | bytes 1540
  69.4 53.4 %copy-start.199 = (s32[128]{0:T(128)S(1)}, s32[128]{0:T(128)}, u32[]{:S(2)}) copy-start(s32[128]{0:T(128)} %get-tuple-element.3685) | copy-start | bytes 1540
  69.4 53.4 %copy-start.201 = (s32[128]{0:T(128)S(1)}, s32[128]{0:T(128)}, u32[]{:S(2)}) copy-start(s32[128]{0:T(128)} %get-tuple-element.3683) | copy-start | bytes 1540
  69.4 53.4 %copy-start.202 = (s32[128]{0:T(128)S(1)}, s32[128]{0:T(128)}, u32[]{:S(2)}) copy-start(s32[128]{0:T(128)} %get-tuple-element.3687) | copy-start | bytes 1540
  69.4 53.4 %copy-start.249 = (pred[128]{0:T(512)(128)(4,1)S(1)}, pred[128]{0:T(512)(128)(4,1)}, u32[]{:S(2)}) copy-start(pred[128]{0:T(512)(128)(4,1)} %fusion.399) | copy-start | bytes 388
  123.5 44.8 %copy-start.154 = (pred[128,64]{0,1:T(8,128)(4,1)}, pred[128,64]{0,1:T(8,128)(4,1)S(1)}, u32[]{:S(2)}) copy-start(pred[128,64]{0,1:T(8,128)(4,1)S(1)} %get-tuple-element.3680) | copy-start | bytes 24580
  124.7 43.6 %copy-start.63 = (f32[6,128,64]{1,2,0:T(8,128)}, f32[6,128,64]{1,2,0:T(8,128)S(1)}, u32[]{:S(2)}) copy-start(f32[6,128,64]{1,2,0:T(8,128)S(1)} %get-tuple-element.3697) | copy-start | bytes 589828
  125.7 42.7 %copy-start.138 = (bf16[1,64,384]{2,1,0:T(8,128)(2,1)}, bf16[1,64,384]{2,1,0:T(8,128)(2,1)S(1)}, u32[]{:S(2)}) copy-start(bf16[1,64,384]{2,1,0:T(8,128)(2,1)S(1)} %get-tuple-element.3627) | copy-start | bytes 147460
  125.8 42.6 %copy-start.142 = (bf16[64,6,64]{2,1,0:T(8,128)(2,1)}, bf16[64,6,64]{2,1,0:T(8,128)(2,1)S(1)}, u32[]{:S(2)}) copy-start(bf16[64,6,64]{2,1,0:T(8,128)(2,1)S(1)} %slice.404) | copy-start | bytes 147460
  183.0 51.5 %copy-start.171 = (f32[6,128]{1,0:T(8,128)}, f32[6,128]{1,0:T(8,128)S(1)}, u32[]{:S(2)}) copy-start(f32[6,128]{1,0:T(8,128)S(1)} %get-tuple-element.3218) | copy-start | bytes 9220
  184.7 463.8 %all-reduce.22.cloned.1.call-start = ((), (), s32[]{:S(2)}) async-start(), calls=%async_computation.13 | async-start | bytes 1572864 | tf_op jit(solution)/shard_map/psum | solution.py:235
  187.0 330.6 %copy-start.39 = (bf16[1,2,64,768]{3,2,1,0:T(8,128)(2,1)}, bf16[1,2,64,768]{3,2,1,0:T(8,128)(2,1)S(1)}, u32[]{:S(2)}) copy-start(bf16[1,2,64,768]{3,2,1,0:T(8,128)(2,1)S(1)} %get-tuple-element.3598) | copy-start | bytes 589828
  235.7 319.4 %copy-start.17 = (bf16[128,6,64]{2,0,1:T(8,128)(2,1)}, bf16[128,6,64]{2,0,1:T(8,128)(2,1)S(1)}, u32[]{:S(2)}) copy-start(bf16[128,6,64]{2,0,1:T(8,128)(2,1)S(1)} %maximum_convert_fusion.3) | copy-start | bytes 294916
  236.9 49.5 %copy-start.58 = (f32[6,128,64]{1,2,0:T(8,128)}, f32[6,128,64]{1,2,0:T(8,128)S(1)}, u32[]{:S(2)}) copy-start(f32[6,128,64]{1,2,0:T(8,128)S(1)} %get-tuple-element.3693) | copy-start | bytes 589828
  354.8 202.9 %copy-start.19 = (bf16[128,6,64]{2,0,1:T(8,128)(2,1)}, bf16[128,6,64]{2,0,1:T(8,128)(2,1)S(1)}, u32[]{:S(2)}) copy-start(bf16[128,6,64]{2,0,1:T(8,128)(2,1)S(1)} %maximum_convert_fusion) | copy-start | bytes 294916
  426.7 46.2 %copy-start.147 = (bf16[64,6,64]{2,0,1:T(8,128)(2,1)}, bf16[64,6,64]{2,0,1:T(8,128)(2,1)S(1)}, u32[]{:S(2)}) copy-start(bf16[64,6,64]{2,0,1:T(8,128)(2,1)S(1)} %get-tuple-element.4259) | copy-start | bytes 147460
  426.7 94.4 %copy-start.112 = (bf16[64,6,64]{2,0,1:T(8,128)(2,1)}, bf16[64,6,64]{2,0,1:T(8,128)(2,1)S(1)}, u32[]{:S(2)}) copy-start(bf16[64,6,64]{2,0,1:T(8,128)(2,1)S(1)} %get-tuple-element.3615) | copy-start | bytes 147460
  472.2 49.8 %copy-start.60 = (f32[6,128,64]{1,2,0:T(8,128)}, f32[6,128,64]{1,2,0:T(8,128)S(1)}, u32[]{:S(2)}) copy-start(f32[6,128,64]{1,2,0:T(8,128)S(1)} %get-tuple-element.3706) | copy-start | bytes 589828
  472.2 49.8 %copy-start.163 = (f32[6,128]{1,0:T(8,128)}, f32[6,128]{1,0:T(8,128)S(1)}, u32[]{:S(2)}) copy-start(f32[6,128]{1,0:T(8,128)S(1)} %broadcast_maximum_fusion.2) | copy-start | bytes 9220
  473.7 48.2 %copy-start.139 = (bf16[1,64,384]{2,1,0:T(8,128)(2,1)}, bf16[1,64,384]{2,1,0:T(8,128)(2,1)S(1)}, u32[]{:S(2)}) copy-start(bf16[1,64,384]{2,1,0:T(8,128)(2,1)S(1)} %get-tuple-element.3623) | copy-start | bytes 147460
  473.9 48.1 %copy-start.141 = (bf16[64,6,64]{2,1,0:T(8,128)(2,1)}, bf16[64,6,64]{2,1,0:T(8,128)(2,1)S(1)}, u32[]{:S(2)}) copy-start(bf16[64,6,64]{2,1,0:T(8,128)(2,1)S(1)} %slice.390) | copy-start | bytes 147460
  553.2 261.7 %all-gather.21.cloned.1.call-start = ((), (), s32[]{:S(2)}) async-start(), calls=%async_computation.5 | async-start | bytes 1671168 | tf_op jit(solution)/shard_map/all_gather | solution.py:333
  555.0 265.1 %all-gather.25.cloned.1.call-start = ((), (), s32[]{:S(2)}) async-start(), calls=%async_computation.8 | async-start | bytes 1671168 | tf_op jit(solution)/shard_map/all_gather | solution.py:333
  555.8 269.5 %all-gather.17.cloned.1.call-start = ((), (), s32[]{:S(2)}) async-start(), calls=%async_computation.3 | async-start | bytes 1671168 | tf_op jit(solution)/shard_map/all_gather | solution.py:333
  557.6 273.0 %all-gather.13.cloned.1.call-start = ((), (), s32[]{:S(2)}) async-start(), calls=%async_computation.1 | async-start | bytes 1671168 | tf_op jit(solution)/shard_map/all_gather | solution.py:333
  558.4 86.5 %copy-start.45 = (bf16[1,2,64,768]{3,2,1,0:T(8,128)(2,1)S(1)}, bf16[1,2,64,768]{3,2,1,0:T(8,128)(2,1)}, u32[]{:S(2)}) copy-start(bf16[1,2,64,768]{3,2,1,0:T(8,128)(2,1)} %get-tuple-element.3596) | copy-start | bytes 589828
  558.5 288.3 %all-gather.23.cloned.1.call-start = ((), (), s32[]{:S(2)}) async-start(), calls=%async_computation.6 | async-start | bytes 1671168 | tf_op jit(solution)/shard_map/all_gather | solution.py:334
  558.5 86.4 %copy-start.4 = (bf16[1536,768]{1,0:T(8,128)(2,1)S(1)}, bf16[1536,768]{1,0:T(8,128)(2,1)}, u32[]{:S(2)}) copy-start(bf16[1536,768]{1,0:T(8,128)(2,1)} %param.55) | copy-start | bytes 7077892
  559.4 39.1 %copy-start.183 = (f32[6,128]{1,0:T(8,128)}, f32[6,128]{1,0:T(8,128)S(1)}, u32[]{:S(2)}) copy-start(f32[6,128]{1,0:T(8,128)S(1)} %log_add_fusion.1) | copy-start | bytes 9220
  599.1 45.8 %copy-start.181 = (f32[6,128]{1,0:T(8,128)}, f32[6,128]{1,0:T(8,128)S(1)}, u32[]{:S(2)}) copy-start(f32[6,128]{1,0:T(8,128)S(1)} %log_add_fusion) | copy-start | bytes 9220
  652.7 92.1 %copy-start.242 = (f32[128]{0:T(128)}, f32[128]{0:T(128)S(1)}, u32[]{:S(2)}) copy-start(f32[128]{0:T(128)S(1)} %negate_multiply_fusion.3) | copy-start | bytes 1540
  653.4 91.3 %copy-start.98 = (bf16[128,1536]{1,0:T(8,128)(2,1)S(1)}, bf16[128,1536]{1,0:T(8,128)(2,1)}, u32[]{:S(2)}) copy-start(bf16[128,1536]{1,0:T(8,128)(2,1)} %copy-done.97) | copy-start | bytes 1179652
  653.4 91.3 %copy-start.133 = (bf16[128,768]{1,0:T(8,128)(2,1)S(1)}, bf16[128,768]{1,0:T(8,128)(2,1)}, u32[]{:S(2)}) copy-start(bf16[128,768]{1,0:T(8,128)(2,1)} %copy-done.132) | copy-start | bytes 589828
  655.2 252.9 %all-reduce.14.cloned.1.call-start = ((), (), s32[]{:S(2)}) async-start(), calls=%async_computation.7 | async-start | bytes 393216 | tf_op jit(solution)/shard_map/psum | solution.py:400
  769.6 50.5 %copy-start.91 = (f32[128,6,32]{2,0,1:T(8,128)}, f32[128,6,32]{2,0,1:T(8,128)S(1)}, u32[]{:S(2)}) copy-start(f32[128,6,32]{2,0,1:T(8,128)S(1)} %get-tuple-element.3231) | copy-start | bytes 294916
  769.6 50.5 %copy-start.94 = (f32[128,6,32]{2,0,1:T(8,128)}, f32[128,6,32]{2,0,1:T(8,128)S(1)}, u32[]{:S(2)}) copy-start(f32[128,6,32]{2,0,1:T(8,128)S(1)} %get-tuple-element.3232) | copy-start | bytes 294916
  892.6 59.1 %all-reduce.20.cloned.1.call-start = ((), (), s32[]{:S(2)}) async-start(), calls=%async_computation.12 | async-start | bytes 1179648 | tf_op jit(solution)/shard_map/psum | solution.py:263
  931.5 253.9 %all-gather.27.cloned.1.call-start = ((), (), s32[]{:S(2)}) async-start(), calls=%async_computation.9 | async-start | bytes 1671168 | tf_op jit(solution)/shard_map/all_gather | solution.py:334
  937.5 21.9 %copy-start.5 = (bf16[1536,768]{1,0:T(8,128)(2,1)S(1)}, bf16[1536,768]{1,0:T(8,128)(2,1)}, u32[]{:S(2)}) copy-start(bf16[1536,768]{1,0:T(8,128)(2,1)} %param.55) | copy-start | bytes 7077892
  958.9 258.3 %all-gather.19.cloned.1.call-start = ((), (), s32[]{:S(2)}) async-start(), calls=%async_computation.4 | async-start | bytes 1671168 | tf_op jit(solution)/shard_map/all_gather | solution.py:334
  978.6 277.0 %all-gather.15.cloned.1.call-start = ((), (), s32[]{:S(2)}) async-start(), calls=%async_computation.2 | async-start | bytes 1671168 | tf_op jit(solution)/shard_map/all_gather | solution.py:334
  984.1 21.2 %copy-start.26 = (bf16[1,1024,384]{2,1,0:T(8,128)(2,1)S(1)}, bf16[1,1024,384]{2,1,0:T(8,128)(2,1)}, u32[]{:S(2)}) copy-start(bf16[1,1024,384]{2,1,0:T(8,128)(2,1)} %all-gather.1) | copy-start | bytes 2359300
  1001.6 324.1 %all-reduce.18.cloned.1.call-start = ((), (), s32[]{:S(2)}) async-start(), calls=%async_computation.11 | async-start | bytes 2752512 | tf_op jit(solution)/shard_map/psum | solution.py:245
  1037.1 144.6 %copy-start.83 = (bf16[128,768]{1,0:T(8,128)(2,1)S(1)}, bf16[128,768]{1,0:T(8,128)(2,1)}, u32[]{:S(2)}) copy-start(bf16[128,768]{1,0:T(8,128)(2,1)} %copy-done.82) | copy-start | bytes 589828
  1049.4 130.5 %copy-start.93 = (f32[128,6,32]{2,0,1:T(8,128)}, f32[128,6,32]{2,0,1:T(8,128)S(1)}, u32[]{:S(2)}) copy-start(f32[128,6,32]{2,0,1:T(8,128)S(1)} %get-tuple-element.3234) | copy-start | bytes 294916
  1049.4 130.5 %copy-start.96 = (f32[128,6,32]{2,0,1:T(8,128)}, f32[128,6,32]{2,0,1:T(8,128)S(1)}, u32[]{:S(2)}) copy-start(f32[128,6,32]{2,0,1:T(8,128)S(1)} %get-tuple-element.3235) | copy-start | bytes 294916
  1051.3 131.8 %copy-start.87 = (bf16[128,768]{1,0:T(8,128)(2,1)S(1)}, bf16[128,768]{1,0:T(8,128)(2,1)}, u32[]{:S(2)}) copy-start(bf16[128,768]{1,0:T(8,128)(2,1)} %copy-done.86) | copy-start | bytes 589828
  1053.2 129.6 %copy-start.89 = (bf16[128,768]{1,0:T(8,128)(2,1)S(1)}, bf16[128,768]{1,0:T(8,128)(2,1)}, u32[]{:S(2)}) copy-start(bf16[128,768]{1,0:T(8,128)(2,1)} %copy-done.88) | copy-start | bytes 589828
  1053.2 129.7 %copy-start.118 = (bf16[128,6,64]{0,2,1:T(8,128)(2,1)S(1)}, bf16[128,6,64]{0,2,1:T(8,128)(2,1)}, u32[]{:S(2)}) copy-start(bf16[128,6,64]{0,2,1:T(8,128)(2,1)} %copy-done.117) | copy-start | bytes 294916
  1309.1 424.2 %all-reduce.16.cloned.1.call-start = ((), (), s32[]{:S(2)}) async-start(), calls=%async_computation.10 | async-start | bytes 28311552 | tf_op jit(solution)/shard_map/psum | solution.py:411
  1317.9 93.8 %copy-start.30 = (bf16[128,768]{1,0:T(8,128)(2,1)S(1)}, bf16[128,768]{1,0:T(8,128)(2,1)}, u32[]{:S(2)}) copy-start(bf16[128,768]{1,0:T(8,128)(2,1)} %all-reduce.12.cloned.1.call-done) | copy-start | bytes 589828
  1317.9 93.8 %copy-start.32 = (bf16[128,768]{1,0:T(8,128)(2,1)S(1)}, bf16[128,768]{1,0:T(8,128)(2,1)}, u32[]{:S(2)}) copy-start(bf16[128,768]{1,0:T(8,128)(2,1)} %get-tuple-element.3478) | copy-start | bytes 589828
  1317.9 93.8 %copy-start.34 = (bf16[128,768]{1,0:T(8,128)(2,1)S(1)}, bf16[128,768]{1,0:T(8,128)(2,1)}, u32[]{:S(2)}) copy-start(bf16[128,768]{1,0:T(8,128)(2,1)} %get-tuple-element.3480) | copy-start | bytes 589828
  1317.9 93.8 %copy-start.36 = (bf16[128,768]{1,0:T(8,128)(2,1)S(1)}, bf16[128,768]{1,0:T(8,128)(2,1)}, u32[]{:S(2)}) copy-start(bf16[128,768]{1,0:T(8,128)(2,1)} %get-tuple-element.3481) | copy-start | bytes 589828
  1328.0 86.6 %copy-start.44 = (bf16[1,2,64,768]{3,2,1,0:T(8,128)(2,1)S(1)}, bf16[1,2,64,768]{3,2,1,0:T(8,128)(2,1)}, u32[]{:S(2)}) copy-start(bf16[1,2,64,768]{3,2,1,0:T(8,128)(2,1)} %get-tuple-element.3595) | copy-start | bytes 589828
  1328.0 86.6 %copy-start.48 = (bf16[1,2,64,768]{3,2,1,0:T(8,128)(2,1)S(1)}, bf16[1,2,64,768]{3,2,1,0:T(8,128)(2,1)}, u32[]{:S(2)}) copy-start(bf16[1,2,64,768]{3,2,1,0:T(8,128)(2,1)} %get-tuple-element.3596) | copy-start | bytes 589828
  1328.0 86.7 %copy-start.54 = (f32[128,768]{1,0:T(8,128)S(1)}, f32[128,768]{1,0:T(8,128)}, u32[]{:S(2)}) copy-start(f32[128,768]{1,0:T(8,128)} %copy-done.53) | copy-start | bytes 1179652
  1328.0 83.7 %copy-start.238 = (f32[128]{0:T(128)}, f32[128]{0:T(128)S(1)}, u32[]{:S(2)}) copy-start(f32[128]{0:T(128)S(1)} %multiply_multiply_fusion.12) | copy-start | bytes 1540
  1328.1 83.6 %copy-start.240 = (f32[128]{0:T(128)}, f32[128]{0:T(128)S(1)}, u32[]{:S(2)}) copy-start(f32[128]{0:T(128)S(1)} %multiply_multiply_fusion.14) | copy-start | bytes 1540
  (231 other events, 1305.8 us)
Sparse Core Ops, SparseCore 0:
  184.8 16.1 all-reduce.11
  553.3 15.6 all-reduce.21
  892.8 15.3 all-reduce.13
  931.6 20.0 all-reduce.19
  1309.2 16.4 all-reduce.17
  1333.6 399.6 all-reduce.15
Sparse Core Ops, SparseCore 1:
  556.8 54.2 all-gather.20
  614.0 55.6 all-gather.24
  672.6 55.3 all-gather.16
  731.1 55.4 all-gather.12
  790.3 56.3 all-gather.22
  958.9 59.3 all-gather.26
  1021.0 56.8 all-gather.18
  1080.5 57.2 all-gather.14
where the time goes:
time: 1770 us; the launch traced here: 1760 us
  blocking collectives  757 us (43%)
  waiting for transfers between devices  360 us (20%)
  matrix products  234 us (13%)
  local copies, waits for them, and re-layouts  230 us (13%)
  other arithmetic  134 us (8%)
  between operations  21.8 us (1%)
    psum x1, waiting for transfers between devices, local(): lax.psum((grad_heads, grad_output, grad_up, grad_bias_up, grad_down, grad...  315 us
    all_gather x4, blocking collectives, local(): key_part = lax.all_gather(clean_keys, 'seq', axis=0, tiled=True)  182 us
    all_gather x4, blocking collectives, local(): lax.all_gather(clean_values, 'seq', axis=0, tiled=True)  173 us
    all_gather x4, blocking collectives, local(): lax.all_gather(row_delta.T, 'seq', axis=0, tiled=True)  163 us
    all_gather x4, blocking collectives, local(): lax.all_gather(log_totals.T, 'seq', axis=0, tiled=True)  158 us
    psum x1, blocking collectives, local(): lax.psum((grad_heads, grad_output, grad_up, grad_bias_up, grad_down, grad...  81 us
    unnamed x526, local copies, waits for them, and re-layouts  73.7 us
  transfers between devices with their start and end apart: 14, of which 5 were waited for; matrix products, arithmetic and copies ran while one was open for 20% of the time, Pallas kernels for 0%

commit v1 on v0

v1 whole, which is shorter than its diff:
```python
import functools
import math

import jax
import jax.numpy as jnp
from jax import lax
from jax.experimental import pallas as pl
from jax.experimental.pallas import tpu as pltpu
from jax.sharding import PartitionSpec as P

HD = 64
LANES = 128
NEG = -1e30
EPS = 1e-05
ROTARY_BASE = 10000.0
GELU_A = math.sqrt(2.0 / math.pi)
GELU_B = 0.044715
MESH = pl.DeviceIdType.MESH
F32 = jnp.float32
BF16 = jnp.bfloat16
WIDE = 256
VMEM_BYTES = 66_000_000


def nn(a, b):
    return lax.dot_general(a, b, (((1,), (0,)), ((), ())), preferred_element_type=F32)


def nt(a, b):
    return lax.dot_general(a, b, (((1,), (1,)), ((), ())), preferred_element_type=F32)


def tn(a, b):
    return lax.dot_general(a, b, (((0,), (0,)), ((), ())), preferred_element_type=F32)


def lane_swap(a):
    lane = lax.broadcasted_iota(jnp.int32, a.shape, 1)
    ahead = pltpu.roll(a, LANES - HD // 2, 1)
    behind = pltpu.roll(a, HD // 2, 1)
    return jnp.where(lane % HD < HD // 2, ahead, behind)


def stack_heads(a):
    lane = lax.broadcasted_iota(jnp.int32, a.shape, 1)
    zero = jnp.zeros_like(a)
    return jnp.concatenate([jnp.where(lane < HD, a, zero), jnp.where(lane >= HD, a, zero)], axis=0)


def merge_heads(a):
    half = a.shape[1] // 2
    sub = lax.broadcasted_iota(jnp.int32, (a.shape[0], half), 0)
    return jnp.where(sub < HD, a[:, :half], a[:, half:])


def fused(dims, *refs):
    n, groups, span, width, head_width, hidden = dims
    (
        x_in, c_in, wh_in, wo_in, wu_in, wd_in, blocks, gain_one, shift_one, gain_two, shift_two,
        bias_up, bias_down, cos_t, sin_t,
        y_out, ig_out, down_out, up_out, heads_out, wout_out, small_out,
        wh, wo, wu, wd, xb, dyb, n1, n2, qs, dos, kv, kvn, dkv, rkv, dkvn, lses, deltas, att, att_f,
        middle, hid, gpre, send_h, recv_h, grad_mid, dq_t,
        acc, arr, small, small_r,
        w_sem, x_send, x_recv, c_send, c_recv, kv_send, kv_recv, h_send, h_recv, g_send, g_recv,
        y_send, y_recv, i_send, i_recv, ar_send, ar_recv, ar_free, sm_send, sm_recv, out_sem,
    ) = refs
    inner = n // groups
    pairs = head_width // LANES
    chunk = 2 * span
    rows = groups * chunk
    stack = 2 * chunk
    key_ranks = min(inner, max(1, WIDE // span))
    key_blocks = inner // key_ranks
    half_rows = rows // 2
    col_tiles = width // LANES
    bits = int(math.log2(n))
    scale = 1.0 / math.sqrt(HD)

    me = lax.axis_index("seq")
    core = lax.axis_index("head")
    group = me // inner
    rank = me % inner

    def peer(seq_index):
        return (seq_index, core)

    sibling = (me, 1 - core)

    def group_peer(step):
        return (group + step) % groups

    def plane_peer(step):
        return (rank + step) % inner

    def remote(src, dst, ssem, rsem, where):
        return pltpu.make_async_remote_copy(
            src_ref=src, dst_ref=dst, send_sem=ssem, recv_sem=rsem, device_id=where, device_id_type=MESH
        )

    barrier = pltpu.get_barrier_semaphore()
    for step in range(1, groups):
        pl.semaphore_signal(barrier, inc=1, device_id=peer(group_peer(step) * inner + rank), device_id_type=MESH)
    for step in range(1, inner):
        pl.semaphore_signal(barrier, inc=1, device_id=peer(group * inner + plane_peer(step)), device_id_type=MESH)
    pl.semaphore_signal(barrier, inc=1, device_id=sibling, device_id_type=MESH)
    weight_copies = [
        pltpu.make_async_copy(wh_in, wh, w_sem.at[0]),
        pltpu.make_async_copy(wo_in, wo, w_sem.at[1]),
        pltpu.make_async_copy(wu_in, wu, w_sem.at[2]),
        pltpu.make_async_copy(wd_in, wd, w_sem.at[3]),
    ]
    own_x = pltpu.make_async_copy(x_in.at[group], xb.at[group], w_sem.at[4])
    own_c = pltpu.make_async_copy(c_in.at[group], dyb.at[group], w_sem.at[5])
    own_x.start()
    weight_copies[0].start()
    pl.semaphore_wait(barrier, groups + inner - 1)

    x_copies, c_copies = [], []
    for step in range(1, groups):
        to = group_peer(step)
        x_copies.append(remote(x_in.at[to], xb.at[group], x_send.at[step], x_recv.at[step], peer(to * inner + rank)))
        c_copies.append(remote(c_in.at[to], dyb.at[group], c_send.at[step], c_recv.at[step], peer(to * inner + rank)))
    for copy in x_copies:
        copy.start()
    for copy in c_copies:
        copy.start()
    for copy in weight_copies[1:]:
        copy.start()
    own_c.start()

    size_b = blocks[group]
    lane_q = lax.broadcasted_iota(jnp.int32, (1, stack), 1)
    in_chunk = lane_q % chunk
    clean_q = in_chunk >= span
    start_q = (in_chunk % span) & (-size_b)
    limit_q = start_q + jnp.where(clean_q, size_b, 0)

    def norm_stats(x):
        center = jnp.mean(x, axis=-1, keepdims=True)
        off = x - center
        inv = lax.rsqrt(jnp.mean(off * off, axis=-1, keepdims=True) + EPS)
        return off * inv, inv

    kv_copies = []

    def project(index):
        x = xb[index].astype(F32)
        hat, _ = norm_stats(x)
        normed = (hat * gain_one[...] + shift_one[...]).astype(BF16)
        n1[pl.ds(pl.multiple_of(index * chunk, chunk), chunk), :] = normed
        slot = index * inner + rank
        cos = cos_t[index]
        sin = sin_t[index]
        cos2 = jnp.concatenate([cos, cos], axis=0)
        sin2 = jnp.concatenate([sin, sin], axis=0)
        at_q = pl.ds(pl.multiple_of(index * stack, stack), stack)
        for kind in range(3):
            out = nn(normed, wh[kind])
            for p in range(pairs):
                part = out[:, p * LANES:(p + 1) * LANES]
                if kind < 2:
                    part = part * cos2 + lane_swap(part) * sin2
                if kind == 0:
                    part = part * scale
                low = part.astype(BF16)
                if kind == 0:
                    qs[p, at_q, :] = stack_heads(low)
                else:
                    where = (kind - 1) * pairs + p
                    kvn[index, where] = low[:span]
                    kv[slot, where] = low[span:]

    for step in range(groups):
        index = group_peer(groups - step) if step else group
        if step == 0:
            own_x.wait()
            weight_copies[0].wait()
        else:
            x_copies[step - 1].wait_recv()
        project(index)
        slot = index * inner + rank
        for near in range(1, inner):
            copy = remote(
                kv.at[slot], kv.at[slot], kv_send.at[index, near], kv_recv.at[index, near],
                peer(group * inner + plane_peer(near)),
            )
            copy.start()

    def kv_wait(index):
        for near in range(1, inner):
            source = index * inner + plane_peer(inner - near)
            remote(
                kv.at[source], kv.at[source], kv_send.at[index, near], kv_recv.at[index, near],
                peer(group * inner + plane_peer(near)),
            ).wait()

    def clean_mask(index, first_rank, count, shape):
        key = lax.broadcasted_iota(jnp.int32, shape, 0) + first_rank * span
        return key < limit_q + rank * span

    def noisy_mask(shape):
        key = lax.broadcasted_iota(jnp.int32, shape, 0) & (-size_b)
        return (key == start_q) & jnp.logical_not(clean_q)

    def head_send(piece, value, which):
        send_h[which % 3, piece * half_rows:(piece + 1) * half_rows, :] = value.astype(BF16)
        copy = head_copy(piece, which)
        copy.start()

    def head_copy(piece, which):
        at = pl.ds(piece * half_rows, half_rows)
        return remote(
            send_h.at[which % 3, at], recv_h.at[which % 3, at], h_send.at[which, piece], h_recv.at[which, piece], sibling
        )

    for index in range(groups):
        kv_wait(index)

        def attend(p, carry, index=index):
            q = qs[p, index * stack:(index + 1) * stack, :]
            pieces = []
            top = None
            for g in range(index + 1):
                keys = kv[g * inner:(g + 1) * inner, p].reshape(inner * span, LANES)
                s = nt(keys, q)
                if g == index:
                    s = jnp.where(clean_mask(index, 0, inner, s.shape), s, NEG)
                pieces.append(s)
                best = jnp.max(s, axis=0, keepdims=True)
                top = best if top is None else jnp.maximum(top, best)
            s = nt(kvn[index, p], q)
            s = jnp.where(noisy_mask(s.shape), s, NEG)
            top = jnp.maximum(top, jnp.max(s, axis=0, keepdims=True))
            e = jnp.exp(s - top)
            total = jnp.sum(e, axis=0, keepdims=True)
            out = tn(kvn[index, pairs + p], e.astype(BF16))
            for g in range(index + 1):
                e = jnp.exp(pieces[g] - top)
                total = total + jnp.sum(e, axis=0, keepdims=True)
                vals = kv[g * inner:(g + 1) * inner, pairs + p].reshape(inner * span, LANES)
                out = out + tn(vals, e.astype(BF16))
            lses[p, :, index * stack:(index + 1) * stack] = top + jnp.log(total)
            rows_out = jnp.transpose(merge_heads(out / total))
            att_f[p, index * chunk:(index + 1) * chunk, :] = rows_out
            at = pl.ds(pl.multiple_of(p * LANES, LANES), LANES)
            att[index * chunk:(index + 1) * chunk, at] = rows_out.astype(BF16)
            return carry

        lax.fori_loop(0, pairs, attend, 0)
        if index == 0:
            weight_copies[1].wait()
        if index % (groups // 2) == groups // 2 - 1:
            piece = index // (groups // 2)
            head_send(piece, nn(att[piece * half_rows:(piece + 1) * half_rows, :], wo[...]), 0)

    def chunk_rows(z):
        return pl.ds(pl.multiple_of(z * chunk, chunk), chunk)

    def second_norm(z, carry):
        at = chunk_rows(z)
        mid = xb[z].astype(F32) + (send_h[0, at, :].astype(F32) + recv_h[0, at, :].astype(F32))
        middle[at, :] = mid
        hat, _ = norm_stats(mid)
        n2[at, :] = (hat * gain_two[...] + shift_two[...]).astype(BF16)
        return carry

    for piece in range(2):
        head_copy(piece, 0).wait()
        lax.fori_loop(piece * groups // 2, (piece + 1) * groups // 2, second_norm, 0)

    weight_copies[2].wait()
    weight_copies[3].wait()
    own_c.wait()
    for copy in c_copies:
        copy.wait_recv()

    up_bias_rows = hidden // WIDE
    small[...] = jnp.zeros_like(small)

    def feed(i, carry):
        cols = pl.ds(pl.multiple_of(i * WIDE, WIDE), WIDE)
        bias = bias_up[pl.ds(i, 1), :]
        sums = jnp.zeros((1, WIDE), F32)
        for part in range(2):
            lo = part * half_rows
            v = nn(n2[lo:lo + half_rows, :], wu[:, cols]) + bias
            dy = dyb[part * groups // 2:(part + 1) * groups // 2].reshape(half_rows, width)
            back = nt(dy, wd[cols, :])
            sq = v * v
            t = jnp.tanh(GELU_A * v * (1.0 + GELU_B * sq))
            half = 0.5 * (1.0 + t)
            hid[lo:lo + half_rows, cols] = (v * half).astype(BF16)
            slope = half + 0.5 * v * (1.0 - t * t) * (GELU_A * (1.0 + 3.0 * GELU_B * sq))
            low = (back * slope).astype(BF16)
            gpre[lo:lo + half_rows, cols] = low
            sums = sums + jnp.sum(low.astype(F32), axis=0, keepdims=True)
        small[pl.ds(i, 1), :] = sums
        dy = dyb[...].reshape(rows, width)
        down = tn(hid[:, cols], dy)
        for c in range(col_tiles):
            at = pl.ds(pl.multiple_of(c * hidden + i * WIDE, WIDE), WIDE)
            acc[0, at, :] = down[:, c * LANES:(c + 1) * LANES].astype(BF16)
        up = tn(n2[...], gpre[:, cols])
        for c in range(WIDE // LANES):
            at = pl.ds(pl.multiple_of((i * (WIDE // LANES) + c) * width, width), width)
            acc[1, at, :] = up[:, c * LANES:(c + 1) * LANES].astype(BF16)
        return carry

    lax.fori_loop(0, up_bias_rows, feed, 0)

    acc_rows = acc.shape[1]
    seg = acc_rows // n
    seg_a = max(16, (seg * 5 // 12 + 8) // 16 * 16)
    seg_sizes = [seg_a, seg_a, seg - 2 * seg_a]
    low_bits = int(math.log2(inner))
    orders = [
        list(range(bits)),
        [1, 0] + list(range(2, bits)),
        list(range(low_bits, bits)) + list(range(low_bits)),
    ]

    def bit_of(bit):
        return (me // (1 << bit)) % 2

    def partner(bit):
        return peer(me + (1 - 2 * bit_of(bit)) * (1 << bit))

    def sum_job(job, part):
        base = n * sum(seg_sizes[:part])
        s = seg_sizes[part]
        order = orders[part]
        lo = 0
        size = n

        def at(ref, first, count):
            return ref.at[job, pl.ds(pl.multiple_of(base + first * s, 16), count * s)]

        for k, bit in enumerate(order):
            half = size // 2
            mine = lo + bit_of(bit) * half
            other = lo + (1 - bit_of(bit)) * half
            copy = remote(
                at(acc, other, half), at(arr, n - size, half),
                ar_send.at[job, part, k], ar_recv.at[job, part, k], partner(bit),
            )
            copy.start()
            yield
            copy.wait()
            pl.semaphore_signal(ar_free.at[job, part, k], inc=1, device_id=partner(bit), device_id_type=MESH)
            step_rows = s

            def add(i, carry, mine=mine, size=size):
                to = pl.ds(pl.multiple_of(base + mine * s + i * step_rows, 16), step_rows)
                frm = pl.ds(pl.multiple_of(base + (n - size) * s + i * step_rows, 16), step_rows)
                acc[job, to, :] = (acc[job, to, :].astype(F32) + arr[job, frm, :].astype(F32)).astype(BF16)
                return carry

            lax.fori_loop(0, half, add, 0)
            lo, size = mine, half
        for k, bit in reversed(list(enumerate(order))):
            pl.semaphore_wait(ar_free.at[job, part, k], 1)
            copy = remote(
                at(acc, lo, size), at(acc, lo, size),
                ar_send.at[job, part, bits + k], ar_recv.at[job, part, bits + k], partner(bit),
            )
            copy.start()
            yield
            copy.wait()
            lo = lo - bit_of(bit) * size
            size = size * 2

    def tick(jobs):
        for job in jobs:
            next(job, None)

    feed_jobs = [sum_job(job, part) for part in range(3) for job in range(2)]
    tick(feed_jobs)

    for piece in range(2):
        lo = piece * half_rows
        head_send(piece, nt(gpre[lo:lo + half_rows, :], wu[...]), 1)
    for piece in range(2):
        lo = piece * half_rows
        head_send(piece, nn(hid[lo:lo + half_rows, :], wd[...]), 2)

    def norm_back(hat, inv, gain, upstream):
        scaled = upstream * gain
        first = jnp.mean(scaled, axis=-1, keepdims=True)
        second = jnp.mean(scaled * hat, axis=-1, keepdims=True)
        return inv * (scaled - first - hat * second)

    def second_back(z, carry):
        gain_sum, shift_sum, bias_sum = carry
        at = chunk_rows(z)
        upstream = send_h[1, at, :].astype(F32) + recv_h[1, at, :].astype(F32)
        hat, inv = norm_stats(middle[at, :])
        dy = dyb[z].astype(F32)
        total = dy + norm_back(hat, inv, gain_two[...], upstream)
        grad_mid[at, :] = total
        n2[at, :] = total.astype(BF16)
        gain_sum = gain_sum + jnp.sum(upstream * hat, axis=0, keepdims=True)
        shift_sum = shift_sum + jnp.sum(upstream, axis=0, keepdims=True)
        bias_sum = bias_sum + jnp.sum(dy, axis=0, keepdims=True)
        return gain_sum, shift_sum, bias_sum

    zero_row = jnp.zeros((1, width), F32)
    sums = (zero_row, zero_row, zero_row)
    for piece in range(2):
        head_copy(piece, 1).wait()
        sums = lax.fori_loop(piece * groups // 2, (piece + 1) * groups // 2, second_back, sums)

    def keep_small(which, row):
        for c in range(width // WIDE):
            at = up_bias_rows + which * (width // WIDE) + c
            small[at:at + 1, :] = row[:, c * WIDE:(c + 1) * WIDE]

    keep_small(0, sums[2])
    keep_small(3, sums[0])
    keep_small(4, sums[1])

    def attended_back(z, carry):
        at = chunk_rows(z)
        back = nt(n2[at, :], wo[...])
        at_q = pl.ds(pl.multiple_of(z * stack, stack), stack)
        for p in range(pairs):
            low = back[:, p * LANES:(p + 1) * LANES].astype(BF16)
            dos[p, at_q, :] = stack_heads(low)
            prod = jnp.transpose(low.astype(F32) * att_f[p, at, :])
            d0 = jnp.sum(prod[:HD], axis=0, keepdims=True)
            d1 = jnp.sum(prod[HD:], axis=0, keepdims=True)
            deltas[p, :, at_q] = jnp.concatenate([d0, d1], axis=1)
        return carry

    lax.fori_loop(0, groups, attended_back, 0)
    tick(feed_jobs)

    def noisy_back(p, carry):
        for index in range(groups):
            at = slice(index * stack, (index + 1) * stack)
            q = qs[p, at, :]
            do = dos[p, at, :]
            keys = kvn[index, p]
            s = nt(keys, q)
            s = jnp.where(noisy_mask(s.shape), s, NEG)
            e = jnp.exp(s - lses[p, :, at])
            dp = nt(kvn[index, pairs + p], do)
            ds = (e * (dp - deltas[p, :, at])).astype(BF16)
            dkvn[index, pairs + p] = nn(e.astype(BF16), do)
            dkvn[index, p] = nn(ds, q)
            dq_t[p, :, at] = tn(keys, ds)
        return carry

    lax.fori_loop(0, pairs, noisy_back, 0)

    def grad_copy(index, near):
        dest = plane_peer(near)
        return remote(
            dkv.at[index * inner + dest], rkv.at[index, near - 1], g_send.at[index, near], g_recv.at[index, near],
            peer(group * inner + dest),
        )

    for index in range(groups):
        for block in range(key_blocks):
            first = index * inner + block * key_ranks

            def clean_back(p, carry, index=index, block=block, first=first):
                at = slice(index * stack, groups * stack)
                q = qs[p, at, :]
                do = dos[p, at, :]
                keys = kv[first:first + key_ranks, p].reshape(key_ranks * span, LANES)
                vals = kv[first:first + key_ranks, pairs + p].reshape(key_ranks * span, LANES)
                s = nt(keys, q)
                own = s[:, :stack]
                own = jnp.where(clean_mask(index, block * key_ranks, key_ranks, own.shape), own, NEG)
                if index < groups - 1:
                    s = jnp.concatenate([own, s[:, stack:]], axis=1)
                else:
                    s = own
                e = jnp.exp(s - lses[p, :, at])
                dp = nt(vals, do)
                ds = (e * (dp - deltas[p, :, at])).astype(BF16)
                dv = nn(e.astype(BF16), do).astype(BF16)
                dk = nn(ds, q).astype(BF16)
                dkv[first:first + key_ranks, p] = dk.reshape(key_ranks, span, LANES)
                dkv[first:first + key_ranks, pairs + p] = dv.reshape(key_ranks, span, LANES)
                dq_t[p, :, at] += tn(keys, ds)
                return carry

            lax.fori_loop(0, pairs, clean_back, 0)
        for near in range(1, inner):
            grad_copy(index, near).start()
        tick(feed_jobs)

    def feed_out(z, carry):
        at = chunk_rows(z)
        fed = send_h[2, at, :].astype(F32) + recv_h[2, at, :].astype(F32)
        dyb[z] = (middle[at, :] + fed + bias_down[...]).astype(BF16)
        return carry

    for piece in range(2):
        head_copy(piece, 2).wait()
    lax.fori_loop(0, groups, feed_out, 0)

    def spread(buf, out, ssem, rsem):
        copies = [pltpu.make_async_copy(buf.at[group], out.at[group], ssem.at[0])]
        for step in range(1, groups):
            to = group_peer(step)
            copies.append(remote(buf.at[to], out.at[group], ssem.at[step], rsem.at[step], peer(to * inner + rank)))
        for copy in copies:
            copy.start()
        return copies

    y_copies = spread(dyb, y_out, y_send, y_recv)

    out_base = 3 * pairs * width
    wout = tn(att[...], n2[...])
    for c in range(col_tiles):
        acc[2, out_base + c * head_width:out_base + (c + 1) * head_width, :] = wout[:, c * LANES:(c + 1) * LANES].astype(BF16)

    for index in range(groups):
        for near in range(1, inner):
            grad_copy(index, near).wait()

    def pre_grads(index, carry):
        cos = cos_t[index]
        sin = sin_t[index]
        cos2 = jnp.concatenate([cos, cos], axis=0)
        sin2 = jnp.concatenate([sin, sin], axis=0)
        at = chunk_rows(index)
        at_q = pl.ds(pl.multiple_of(index * stack, stack), stack)
        slot = index * inner + rank
        for p in range(pairs):
            gq = jnp.transpose(merge_heads(dq_t[p, :, at_q])) * scale
            gq = gq * cos2 - lane_swap(gq) * sin2
            gpre[at, p * LANES:(p + 1) * LANES] = gq.astype(BF16)
            for kind in range(2):
                which = kind * pairs + p
                total = dkv[slot, which].astype(F32)
                for near in range(inner - 1):
                    total = total + rkv[index, near, which].astype(F32)
                g = jnp.concatenate([dkvn[index, which], total], axis=0)
                if kind == 0:
                    g = g * cos2 - lane_swap(g) * sin2
                col = (kind + 1) * head_width + p * LANES
                gpre[at, col:col + LANES] = g.astype(BF16)
        return carry

    lax.fori_loop(0, groups, pre_grads, 0)

    for piece in range(2):
        lo = piece * half_rows
        back = nt(gpre[lo:lo + half_rows, :head_width], wh[0])
        back = back + nt(gpre[lo:lo + half_rows, head_width:2 * head_width], wh[1])
        back = back + nt(gpre[lo:lo + half_rows, 2 * head_width:3 * head_width], wh[2])
        head_send(piece, back, 3)

    for kind in range(3):
        part = tn(n1[...], gpre[:, kind * head_width:(kind + 1) * head_width])
        for p in range(pairs):
            at = (kind * pairs + p) * width
            acc[2, at:at + width, :] = part[:, p * LANES:(p + 1) * LANES].astype(BF16)
    tick(feed_jobs)
    head_jobs = [sum_job(2, part) for part in range(3)]
    tick(head_jobs)

    def first_back(z, carry):
        gain_sum, shift_sum = carry
        at = chunk_rows(z)
        upstream = send_h[0, at, :].astype(F32) + recv_h[0, at, :].astype(F32)
        hat, inv = norm_stats(xb[z].astype(F32))
        dyb[z] = (grad_mid[at, :] + norm_back(hat, inv, gain_one[...], upstream)).astype(BF16)
        gain_sum = gain_sum + jnp.sum(upstream * hat, axis=0, keepdims=True)
        shift_sum = shift_sum + jnp.sum(upstream, axis=0, keepdims=True)
        return gain_sum, shift_sum

    for copy in y_copies:
        copy.wait()
    sums = (zero_row, zero_row)
    for piece in range(2):
        head_copy(piece, 3).wait()
        sums = lax.fori_loop(piece * groups // 2, (piece + 1) * groups // 2, first_back, sums)
    ig_copies = spread(dyb, ig_out, i_send, i_recv)
    keep_small(1, sums[0])
    keep_small(2, sums[1])

    def small_job():
        for bit in range(bits):
            copy = remote(small.at[...], small_r.at[bit], sm_send.at[bit], sm_recv.at[bit], partner(bit))
            copy.start()
            yield
            copy.wait()
            small[...] = small[...] + small_r[bit]

    last = [small_job()]
    all_jobs = feed_jobs + head_jobs + last
    for _ in range(2 * bits + 1):
        tick(all_jobs)
    small_out[...] = small[...]

    outs = []
    for c in range(col_tiles):
        at = slice(c * LANES, (c + 1) * LANES)
        outs.append((acc.at[0, pl.ds(c * hidden, hidden)], down_out.at[:, at]))
    for c in range(hidden // LANES):
        at = slice(c * LANES, (c + 1) * LANES)
        outs.append((acc.at[1, pl.ds(c * width, width)], up_out.at[:, at]))
    for kind in range(3):
        for p in range(pairs):
            at = slice(p * LANES, (p + 1) * LANES)
            outs.append((acc.at[2, pl.ds((kind * pairs + p) * width, width)], heads_out.at[kind, :, at]))
    for c in range(col_tiles):
        at = slice(c * LANES, (c + 1) * LANES)
        outs.append((acc.at[2, pl.ds(out_base + c * head_width, head_width)], wout_out.at[:, at]))
    copies = [pltpu.make_async_copy(src, dst, out_sem.at[i]) for i, (src, dst) in enumerate(outs)]
    for copy in copies:
        copy.start()
    for copy in x_copies + c_copies:
        copy.wait_send()
    for copy in ig_copies:
        copy.wait()
    for copy in copies:
        copy.wait()


def local(
    layer_input, block_sizes, mixing_gain, mixing_shift, w_heads, w_output, feed_gain, feed_shift,
    w_up, bias_up, w_down, bias_down, cotangent,
):
    groups, _, span, width = layer_input.shape
    n = lax.axis_size("seq")
    head_width = w_heads.shape[2]
    hidden = w_up.shape[1]
    inner = n // groups
    pairs = head_width // LANES
    chunk = 2 * span
    rows = groups * chunk
    stack = 2 * chunk
    rank = lax.axis_index("seq") % inner
    bits = int(math.log2(n))

    first = (jnp.arange(groups, dtype=jnp.int32) * inner + rank) * span
    positions = (first[:, None] + jnp.arange(span, dtype=jnp.int32)[None, :]).astype(F32)
    lane = jnp.arange(LANES, dtype=jnp.int32)
    half = HD // 2
    frequency = jnp.exp((lane % half).astype(F32) * (-math.log(ROTARY_BASE) / half))
    angles = positions[:, :, None] * frequency[None, None, :]
    cos_t = jnp.cos(angles)
    sin_t = jnp.sin(angles) * jnp.where(lane % HD < half, -1.0, 1.0).astype(F32)

    acc_rows = hidden * width // LANES
    small_rows = (hidden // WIDE + 5 * (width // WIDE) + 7) // 8 * 8
    out_copies = width // LANES + hidden // LANES + 3 * pairs + width // LANES
    anywhere = pl.BlockSpec(memory_space=pl.ANY)
    vmem = pl.BlockSpec(memory_space=pltpu.VMEM)
    dma = pltpu.SemaphoreType.DMA
    scratch = [
        pltpu.VMEM((3, width, head_width), BF16),
        pltpu.VMEM((head_width, width), BF16),
        pltpu.VMEM((width, hidden), BF16),
        pltpu.VMEM((hidden, width), BF16),
        pltpu.VMEM((groups, chunk, width), BF16),
        pltpu.VMEM((groups, chunk, width), BF16),
        pltpu.VMEM((rows, width), BF16),
        pltpu.VMEM((rows, width), BF16),
        pltpu.VMEM((pairs, groups * stack, LANES), BF16),
        pltpu.VMEM((pairs, groups * stack, LANES), BF16),
        pltpu.VMEM((n, 2 * pairs, span, LANES), BF16),
        pltpu.VMEM((groups, 2 * pairs, span, LANES), BF16),
        pltpu.VMEM((n, 2 * pairs, span, LANES), BF16),
        pltpu.VMEM((groups, inner - 1, 2 * pairs, span, LANES), BF16),
        pltpu.VMEM((groups, 2 * pairs, span, LANES), F32),
        pltpu.VMEM((pairs, 1, groups * stack), F32),
        pltpu.VMEM((pairs, 1, groups * stack), F32),
        pltpu.VMEM((rows, head_width), BF16),
        pltpu.VMEM((pairs, rows, LANES), F32),
        pltpu.VMEM((rows, width), F32),
        pltpu.VMEM((rows, hidden), BF16),
        pltpu.VMEM((rows, hidden), BF16),
        pltpu.VMEM((3, rows, width), BF16),
        pltpu.VMEM((3, rows, width), BF16),
        pltpu.VMEM((rows, width), F32),
        pltpu.VMEM((pairs, LANES, groups * stack), F32),
        pltpu.VMEM((3, acc_rows, LANES), BF16),
        pltpu.VMEM((3, acc_rows, LANES), BF16),
        pltpu.VMEM((small_rows, WIDE), F32),
        pltpu.VMEM((bits, small_rows, WIDE), F32),
        dma((6,)),
        dma((groups,)), dma((groups,)), dma((groups,)), dma((groups,)),
        dma((groups, inner)), dma((groups, inner)),
        dma((4, 2)), dma((4, 2)),
        dma((groups, inner)), dma((groups, inner)),
        dma((groups,)), dma((groups,)), dma((groups,)), dma((groups,)),
        dma((3, 3, 2 * bits)), dma((3, 3, 2 * bits)), pltpu.SemaphoreType.REGULAR((3, 3, bits)),
        dma((bits,)), dma((bits,)),
        dma((out_copies,)),
    ]
    out_shape = (
        jax.ShapeDtypeStruct((groups, chunk, width), BF16),
        jax.ShapeDtypeStruct((groups, chunk, width), BF16),
        jax.ShapeDtypeStruct((hidden, width), BF16),
        jax.ShapeDtypeStruct((width, hidden), BF16),
        jax.ShapeDtypeStruct((3, width, head_width), BF16),
        jax.ShapeDtypeStruct((head_width, width), BF16),
        jax.ShapeDtypeStruct((small_rows, WIDE), F32),
    )
    y, ig, down, up, heads, wout, small = pl.pallas_call(
        functools.partial(fused, (n, groups, span, width, head_width, hidden)),
        out_shape=out_shape,
        in_specs=[anywhere] * 6 + [pl.BlockSpec(memory_space=pltpu.SMEM)] + [vmem] * 8,
        out_specs=(anywhere,) * 6 + (vmem,),
        scratch_shapes=scratch,
        compiler_params=pltpu.CompilerParams(
            collective_id=0, has_side_effects=True, vmem_limit_bytes=VMEM_BYTES
        ),
    )(
        layer_input.reshape(groups, chunk, width),
        cotangent.reshape(groups, chunk, width),
        w_heads, w_output, w_up, w_down, block_sizes,
        mixing_gain[None], mixing_shift[None], feed_gain[None], feed_shift[None],
        bias_up.reshape(hidden // WIDE, WIDE), bias_down[None], cos_t, sin_t,
    )
    up_rows = hidden // WIDE
    per = width // WIDE

    def vector(i):
        return small[up_rows + i * per:up_rows + (i + 1) * per].reshape(width)

    full = (groups, 2, span, width)
    return (
        y.reshape(full),
        ig.astype(F32).reshape(full),
        heads.astype(F32),
        wout.astype(F32),
        up.astype(F32),
        small[:up_rows].reshape(hidden),
        down.astype(F32),
        vector(0),
        vector(1),
        vector(2),
        vector(3),
        vector(4),
    )


def solution(mesh):
    in_specs = (
        P(None, None, "seq", None), P(), P(), P(), P(None, None, "head"), P("head", None), P(), P(),
        P(None, "head"), P("head"), P("head", None), P(), P(None, None, "seq", None),
    )
    out_specs = (
        P(None, None, "seq", None), P(None, None, "seq", None), P(None, None, "head"), P("head", None),
        P(None, "head"), P("head"), P("head", None), P(), P(), P(), P(), P(),
    )
    return jax.shard_map(local, mesh=mesh, in_specs=in_specs, out_specs=out_specs, check_vma=False)
```

time: 1770 us -> 255 us (0.14)
  blocking collectives: 757 us -> 0 us
  waiting for transfers between devices: 360 us -> 0 us
  matrix products: 234 us -> 0 us
  Pallas kernels: 0 us -> 229 us
  local copies, waits for them, and re-layouts: 230 us -> 12.1 us
  other arithmetic: 134 us -> 12.9 us
  between operations: 21.8 us -> 0.7 us
    all_gather x16 -> x0, blocking collectives: 676 us -> none  [the longest x4 182 us: local(): key_part = lax.all_gather(clean_keys, 'seq', axis=0, tiled=True)]
    psum x6 -> x0, waiting for transfers between devices: 349 us -> none  [the longest x1 315 us: local(): lax.psum((grad_heads, grad_output, grad_up, grad_bias_up, grad_down, grad...]
    dot_general x112 -> x0, matrix products: 234 us -> none  [the longest x12 29.8 us: block_gradients(): jnp.einsum('qhd,khd->hqk', query_part, key_part, preferred_element_type=j...]
    pallas_call x0 -> x1, Pallas kernels: none -> 229 us  [local(): pl.pallas_call(functools.partial(fused, (n, groups, span, width, head_wid...]
    psum x1 -> x0, blocking collectives: 81 us -> none  [local(): lax.psum((grad_heads, grad_output, grad_up, grad_bias_up, grad_down, grad...]
    unnamed x526 -> x13, local copies, waits for them, and re-layouts: 73.7 us -> 0.9 us
    another operation x28 -> x0, local copies, waits for them, and re-layouts: 31.1 us -> none
    reduce_sum x25 -> x0, other arithmetic: 30.6 us -> none  [the longest x5 11.7 us: layer_norm(): return offsets * lax.rsqrt(spread + norm_eps) * norm_gain + norm_shift]
  transfers between devices with their start and end apart: 14 -> 0, of which waited for: 5 -> 0; matrix products, arithmetic and copies ran while one was open for 20% -> 0% of each run, Pallas kernels for 0% -> 0%
where the time goes in v1:
time: 255 us; the launch traced here: 254 us
  Pallas kernels  229 us (90%)
  other arithmetic  12.9 us (5%)
  local copies, waits for them, and re-layouts  12.1 us (5%)
    pallas_call x1, Pallas kernels, local(): pl.pallas_call(functools.partial(fused, (n, groups, span, width, head_wid...  229 us

profile of v1, /device:TPU:0, one launch (start us, length us, event | category | flops | bytes accessed | tf_op | source)
XLA Modules:
  0.0 254.5 jit_solution(10577184220891078235)
XLA Ops:
  0.7 0.1 add_convert_fusion
  0.7 1.2 fusion
  2.0 1.3 reshape.112.refs_11_
  3.3 1.3 broadcast_in_dim.28.refs_7_
  4.6 1.3 broadcast_in_dim.29.refs_8_
  5.8 1.3 broadcast_in_dim.30.refs_9_
  7.1 1.3 broadcast_in_dim.31.refs_10_
  8.4 1.3 broadcast_in_dim.32.refs_12_
  9.6 228.7 %shard_map.220 = (bf16[4,128,768]{2,1,0:T(8,128)(2,1)}, bf16[4,128,768]{2,1,0:T(8,128)(2,1)}, bf16[1536,768]{1,0:T(8,128)(2,1)}, bf16[768,1536]{1,0:T(8,128)(2,1...) custom-call(bf16[4,128,768]{2,1,0:T(8,128)(2,1)} %bitcast.5, ...), custom_call_target="tpu_custom_call" | custom-call | tf_op jit(solution)/shard_map/pallas_call | solution.py:707
  238.3 0.0 copy-start
  238.3 4.6 %convert_element_type.31 = f32[768,1536]{1,0:T(8,128)} convert(bf16[768,1536]{1,0:T(8,128)(2,1)} %get-tuple-element.23) | non-fusion elementwise | flops 1179648 | bytes 7077888 | tf_op jit(solution)/shard_map/convert_element_type | solution.py:735
  243.0 0.0 copy-done
  243.0 0.0 copy-start.1
  243.0 2.5 %convert_element_type.32 = f32[1536,768]{1,0:T(8,128)} convert(bf16[1536,768]{1,0:T(8,128)(2,1)S(1)} %copy-done) | non-fusion elementwise | flops 1179648 | bytes 7077888 | tf_op jit(solution)/shard_map/convert_element_type | solution.py:737
  245.5 0.0 copy-done.1
  245.5 0.0 copy-start.3
  245.5 2.0 convert_element_type.29
  247.6 0.0 copy-start.4
  247.6 0.0 copy-start.5
  247.6 0.0 copy-start.2
  247.6 0.0 copy-done.3
  247.6 1.3 convert.1
  248.9 0.0 copy-done.4
  248.9 1.1 convert_element_type.30
  250.0 0.0 copy-done.5
  250.0 0.6 reshape.117
  250.6 0.6 reshape.118
  251.2 0.6 reshape.119
  251.8 0.6 reshape.120
  252.4 0.6 reshape.121
  253.0 0.6 reshape.116
  253.6 0.0 copy-done.2
  253.6 0.9 copy.26
  (4 shorter events, 0.0 us)
Async XLA Ops:
  238.3 4.7 %copy-start = (bf16[1536,768]{1,0:T(8,128)(2,1)S(1)}, bf16[1536,768]{1,0:T(8,128)(2,1)}, u32[]{:S(2)}) copy-start(bf16[1536,768]{1,0:T(8,128)(2,1)} %get-tuple-element.25) | copy-start | bytes 7077892
  243.0 2.5 %copy-start.1 = (bf16[3,768,384]{2,1,0:T(8,128)(2,1)S(1)}, bf16[3,768,384]{2,1,0:T(8,128)(2,1)}, u32[]{:S(2)}) copy-start(bf16[3,768,384]{2,1,0:T(8,128)(2,1)} %get-tuple-element.21) | copy-start | bytes 5308420
  245.5 2.0 copy-start.3
  247.6 1.3 copy-start.4
  247.6 2.4 copy-start.5
  247.6 6.0 %copy-start.2 = (bf16[4,128,768]{2,1,0:T(8,128)(2,1)S(1)}, bf16[4,128,768]{2,1,0:T(8,128)(2,1)}, u32[]{:S(2)}) copy-start(bf16[4,128,768]{2,1,0:T(8,128)(2,1)} %get-tuple-element.19) | copy-start | bytes 2359300

commit v2 on v1

--- a/solution.py
+++ b/solution.py
@@ -53,19 +53,26 @@
     return jnp.where(sub < HD, a[:, :half], a[:, half:])
 
 
+def job_layout(n, width, head_width, hidden):
+    whole = [hidden * width // LANES] * 2 + [2 * head_width * width // LANES] * 2
+    padded = [-(-count // (16 * n)) * 16 * n for count in whole]
+    return padded, [sum(padded[:i]) for i in range(len(padded) + 1)]
+
+
 def fused(dims, *refs):
     n, groups, span, width, head_width, hidden = dims
     (
-        x_in, c_in, wh_in, wo_in, wu_in, wd_in, blocks, gain_one, shift_one, gain_two, shift_two,
-        bias_up, bias_down, cos_t, sin_t,
+        x_in, c_in, wh_in, wo_in, wu_in, wd_in, blocks,
+        gain_one_in, shift_one_in, gain_two_in, shift_two_in, bias_up_in, bias_down_in,
         y_out, ig_out, down_out, up_out, heads_out, wout_out, small_out,
         wh, wo, wu, wd, xb, dyb, n1, n2, qs, dos, kv, kvn, dkv, rkv, dkvn, lses, deltas, att, att_f,
         middle, hid, gpre, send_h, recv_h, grad_mid, dq_t,
-        acc, arr, small, small_r,
-        w_sem, x_send, x_recv, c_send, c_recv, kv_send, kv_recv, h_send, h_recv, g_send, g_recv,
-        y_send, y_recv, i_send, i_recv, ar_send, ar_recv, ar_free, sm_send, sm_recv, out_sem,
+        acc, arr, small, small_r, cos_t, sin_t, bias_rows, vectors,
+        w_sem, x_send, x_recv, c_send, c_recv, xf_send, xf_recv, cf_send, cf_recv, kv_send, kv_recv, h_send, h_recv, g_send, g_recv,
+        y_send, y_recv, i_send, i_recv, yf_send, yf_recv, if_send, if_recv, ar_send, ar_recv, ar_free, sm_send, sm_recv, out_sem,
     ) = refs
     inner = n // groups
+    job_rows, bases = job_layout(n, width, head_width, hidden)
     pairs = head_width // LANES
     chunk = 2 * span
     rows = groups * chunk
@@ -76,6 +83,8 @@
     col_tiles = width // LANES
     bits = int(math.log2(n))
     scale = 1.0 / math.sqrt(HD)
+    up_bias_rows = hidden // WIDE
+    gain_one, shift_one, gain_two, shift_two, bias_down = (vectors.at[i:i + 1, :] for i in range(5))
 
     me = lax.axis_index("seq")
     core = lax.axis_index("head")
@@ -116,14 +125,25 @@
     weight_copies[0].start()
     pl.semaphore_wait(barrier, groups + inner - 1)
 
-    x_copies, c_copies = [], []
+    x_copies, c_copies, x_passes, c_passes = [], [], [], []
+    share = pl.ds(pl.multiple_of(core * span, span), span)
     for step in range(1, groups):
         to = group_peer(step)
-        x_copies.append(remote(x_in.at[to], xb.at[group], x_send.at[step], x_recv.at[step], peer(to * inner + rank)))
-        c_copies.append(remote(c_in.at[to], dyb.at[group], c_send.at[step], c_recv.at[step], peer(to * inner + rank)))
+        source = group_peer(groups - step)
+        where = peer(to * inner + rank)
+        x_copies.append(
+            remote(x_in.at[to, share], xb.at[group, share], x_send.at[step], x_recv.at[step], where)
+        )
+        c_copies.append(
+            remote(c_in.at[to, share], dyb.at[group, share], c_send.at[step], c_recv.at[step], where)
+        )
+        x_passes.append(
+            remote(xb.at[source, share], xb.at[source, share], xf_send.at[step], xf_recv.at[step], sibling)
+        )
+        c_passes.append(
+            remote(dyb.at[source, share], dyb.at[source, share], cf_send.at[step], cf_recv.at[step], sibling)
+        )
     for copy in x_copies:
-        copy.start()
-    for copy in c_copies:
         copy.start()
     for copy in weight_copies[1:]:
         copy.start()
@@ -142,7 +162,22 @@
         inv = lax.rsqrt(jnp.mean(off * off, axis=-1, keepdims=True) + EPS)
         return off * inv, inv
 
-    kv_copies = []
+    for row in range(up_bias_rows):
+        bias_rows[row:row + 1, :] = bias_up_in[row * WIDE:(row + 1) * WIDE].reshape(1, WIDE)
+    for row, vector in enumerate((gain_one_in, shift_one_in, gain_two_in, shift_two_in, bias_down_in)):
+        vectors[row:row + 1, :] = vector[...].reshape(1, width)
+
+    half_head = HD // 2
+    lane = lax.broadcasted_iota(jnp.int32, (1, LANES), 1)
+    frequency = jnp.exp((lane % half_head).astype(F32) * (-math.log(ROTARY_BASE) / half_head))
+    sign = jnp.where(lane % HD < half_head, -1.0, 1.0)
+    for index in range(groups):
+        start = (index * inner + rank) * span
+        position = lax.broadcasted_iota(jnp.int32, (span, LANES), 0) + start
+        angle = position.astype(F32) * frequency
+        cos_t[index] = jnp.cos(angle)
+        sin_t[index] = jnp.sin(angle) * sign
+
 
     def project(index):
         x = xb[index].astype(F32)
@@ -177,8 +212,14 @@
             own_x.wait()
             weight_copies[0].wait()
         else:
-            x_copies[step - 1].wait_recv()
+            x_passes[step - 1].wait()
         project(index)
+        if step == 0:
+            for copy, onward in zip(x_copies, x_passes):
+                copy.wait_recv()
+                onward.start()
+            for copy in c_copies:
+                copy.start()
         slot = index * inner + rank
         for near in range(1, inner):
             copy = remote(
@@ -202,6 +243,22 @@
     def noisy_mask(shape):
         key = lax.broadcasted_iota(jnp.int32, shape, 0) & (-size_b)
         return (key == start_q) & jnp.logical_not(clean_q)
+
+    own_c.wait()
+    for copy, onward in zip(c_copies, c_passes):
+        copy.wait_recv()
+        onward.start()
+    weight_copies[2].wait()
+    weight_copies[3].wait()
+    for copy in c_passes:
+        copy.wait()
+
+    def feed_back(i, carry):
+        cols = pl.ds(pl.multiple_of(i * WIDE, WIDE), WIDE)
+        gpre[:, cols] = nt(dyb[...].reshape(rows, width), wd[cols, :]).astype(BF16)
+        return carry
+
+    lax.fori_loop(0, up_bias_rows, feed_back, 0)
 
     def head_send(piece, value, which):
         send_h[which % 3, piece * half_rows:(piece + 1) * half_rows, :] = value.astype(BF16)
@@ -269,24 +326,17 @@
         head_copy(piece, 0).wait()
         lax.fori_loop(piece * groups // 2, (piece + 1) * groups // 2, second_norm, 0)
 
-    weight_copies[2].wait()
-    weight_copies[3].wait()
-    own_c.wait()
-    for copy in c_copies:
-        copy.wait_recv()
-
-    up_bias_rows = hidden // WIDE
     small[...] = jnp.zeros_like(small)
 
     def feed(i, carry):
         cols = pl.ds(pl.multiple_of(i * WIDE, WIDE), WIDE)
-        bias = bias_up[pl.ds(i, 1), :]
+        bias = bias_rows[pl.ds(i, 1), :]
+        dy = dyb[...].reshape(rows, width)
         sums = jnp.zeros((1, WIDE), F32)
         for part in range(2):
             lo = part * half_rows
             v = nn(n2[lo:lo + half_rows, :], wu[:, cols]) + bias
-            dy = dyb[part * groups // 2:(part + 1) * groups // 2].reshape(half_rows, width)
-            back = nt(dy, wd[cols, :])
+            back = gpre[lo:lo + half_rows, cols].astype(F32)
             sq = v * v
             t = jnp.tanh(GELU_A * v * (1.0 + GELU_B * sq))
             half = 0.5 * (1.0 + t)
@@ -296,23 +346,20 @@
             gpre[lo:lo + half_rows, cols] = low
             sums = sums + jnp.sum(low.astype(F32), axis=0, keepdims=True)
         small[pl.ds(i, 1), :] = sums
-        dy = dyb[...].reshape(rows, width)
         down = tn(hid[:, cols], dy)
         for c in range(col_tiles):
             at = pl.ds(pl.multiple_of(c * hidden + i * WIDE, WIDE), WIDE)
-            acc[0, at, :] = down[:, c * LANES:(c + 1) * LANES].astype(BF16)
+            acc[at, :] = down[:, c * LANES:(c + 1) * LANES].astype(BF16)
+        return carry
+
+    def feed_up(i, carry):
+        cols = pl.ds(pl.multiple_of(i * WIDE, WIDE), WIDE)
         up = tn(n2[...], gpre[:, cols])
         for c in range(WIDE // LANES):
-            at = pl.ds(pl.multiple_of((i * (WIDE // LANES) + c) * width, width), width)
-            acc[1, at, :] = up[:, c * LANES:(c + 1) * LANES].astype(BF16)
+            at = pl.ds(pl.multiple_of(bases[1] + (i * (WIDE // LANES) + c) * width, LANES), width)
+            acc[at, :] = up[:, c * LANES:(c + 1) * LANES].astype(BF16)
         return carry
 
-    lax.fori_loop(0, up_bias_rows, feed, 0)
-
-    acc_rows = acc.shape[1]
-    seg = acc_rows // n
-    seg_a = max(16, (seg * 5 // 12 + 8) // 16 * 16)
-    seg_sizes = [seg_a, seg_a, seg - 2 * seg_a]
     low_bits = int(math.log2(inner))
     orders = [
         list(range(bits)),
@@ -326,15 +373,18 @@
     def partner(bit):
         return peer(me + (1 - 2 * bit_of(bit)) * (1 << bit))
 
-    def sum_job(job, part):
-        base = n * sum(seg_sizes[:part])
-        s = seg_sizes[part]
+    def sum_steps(job, part):
+        seg = job_rows[job] // n
+        first = max(16, int(seg * 0.4 / 16 + 0.5) * 16)
+        sizes = [first, first, seg - 2 * first]
+        base = bases[job] + n * sum(sizes[:part])
+        s = sizes[part]
         order = orders[part]
         lo = 0
         size = n
 
         def at(ref, first, count):
-            return ref.at[job, pl.ds(pl.multiple_of(base + first * s, 16), count * s)]
+            return ref.at[pl.ds(pl.multiple_of(base + first * s, 16), count * s)]
 
         for k, bit in enumerate(order):
             half = size // 2
@@ -348,12 +398,11 @@
             yield
             copy.wait()
             pl.semaphore_signal(ar_free.at[job, part, k], inc=1, device_id=partner(bit), device_id_type=MESH)
-            step_rows = s
 
             def add(i, carry, mine=mine, size=size):
-                to = pl.ds(pl.multiple_of(base + mine * s + i * step_rows, 16), step_rows)
-                frm = pl.ds(pl.multiple_of(base + (n - size) * s + i * step_rows, 16), step_rows)
-                acc[job, to, :] = (acc[job, to, :].astype(F32) + arr[job, frm, :].astype(F32)).astype(BF16)
+                to = pl.ds(pl.multiple_of(base + mine * s + i * s, 16), s)
+                frm = pl.ds(pl.multiple_of(base + (n - size) * s + i * s, 16), s)
+                acc[to, :] = (acc[to, :].astype(F32) + arr[frm, :].astype(F32)).astype(BF16)
                 return carry
 
             lax.fori_loop(0, half, add, 0)
@@ -370,12 +419,17 @@
             lo = lo - bit_of(bit) * size
             size = size * 2
 
-    def tick(jobs):
-        for job in jobs:
-            next(job, None)
-
-    feed_jobs = [sum_job(job, part) for part in range(3) for job in range(2)]
-    tick(feed_jobs)
+    jobs = [[sum_steps(job, part) for part in range(3)] for job in range(len(job_rows))]
+
+    def tick(*which):
+        for job in which:
+            for steps in jobs[job]:
+                next(steps, None)
+
+    lax.fori_loop(0, up_bias_rows, feed, 0)
+    tick(0)
+    lax.fori_loop(0, up_bias_rows, feed_up, 0)
+    tick(1)
 
     for piece in range(2):
         lo = piece * half_rows
@@ -433,7 +487,12 @@
         return carry
 
     lax.fori_loop(0, groups, attended_back, 0)
-    tick(feed_jobs)
+    tick(0, 1)
+
+    wout = tn(att[...], n2[...])
+    for c in range(col_tiles):
+        at = bases[2] + c * head_width
+        acc[at:at + head_width, :] = wout[:, c * LANES:(c + 1) * LANES].astype(BF16)
 
     def noisy_back(p, carry):
         for index in range(groups):
@@ -490,7 +549,7 @@
             lax.fori_loop(0, pairs, clean_back, 0)
         for near in range(1, inner):
             grad_copy(index, near).start()
-        tick(feed_jobs)
+        tick(0, 1)
 
     def feed_out(z, carry):
         at = chunk_rows(z)
@@ -502,38 +561,49 @@
         head_copy(piece, 2).wait()
     lax.fori_loop(0, groups, feed_out, 0)
 
-    def spread(buf, out, ssem, rsem):
-        copies = [pltpu.make_async_copy(buf.at[group], out.at[group], ssem.at[0])]
+    def spread(buf, out, ssem, rsem, psend, precv):
+        copies, passes = [], []
+        own = pltpu.make_async_copy(buf.at[group], out.at[group], ssem.at[0])
+        own.start()
         for step in range(1, groups):
             to = group_peer(step)
-            copies.append(remote(buf.at[to], out.at[group], ssem.at[step], rsem.at[step], peer(to * inner + rank)))
+            source = group_peer(groups - step)
+            copies.append(
+                remote(buf.at[to, share], out.at[group, share], ssem.at[step], rsem.at[step], peer(to * inner + rank))
+            )
+            passes.append(remote(out.at[source, share], out.at[source, share], psend.at[step], precv.at[step], sibling))
         for copy in copies:
             copy.start()
-        return copies
-
-    y_copies = spread(dyb, y_out, y_send, y_recv)
-
-    out_base = 3 * pairs * width
-    wout = tn(att[...], n2[...])
-    for c in range(col_tiles):
-        acc[2, out_base + c * head_width:out_base + (c + 1) * head_width, :] = wout[:, c * LANES:(c + 1) * LANES].astype(BF16)
-
-    for index in range(groups):
-        for near in range(1, inner):
-            grad_copy(index, near).wait()
-
-    def pre_grads(index, carry):
+        return own, copies, passes
+
+    def pass_on(spread_out):
+        own, copies, passes = spread_out
+        own.wait()
+        for copy, onward in zip(copies, passes):
+            copy.wait()
+            onward.start()
+
+    y_spread = spread(dyb, y_out, y_send, y_recv, yf_send, yf_recv)
+
+    def turned(index, grad):
         cos = cos_t[index]
         sin = sin_t[index]
         cos2 = jnp.concatenate([cos, cos], axis=0)
         sin2 = jnp.concatenate([sin, sin], axis=0)
+        return grad * cos2 - lane_swap(grad) * sin2
+
+    def query_grads(index, carry):
         at = chunk_rows(index)
         at_q = pl.ds(pl.multiple_of(index * stack, stack), stack)
+        for p in range(pairs):
+            gq = jnp.transpose(merge_heads(dq_t[p, :, at_q])) * scale
+            gpre[at, p * LANES:(p + 1) * LANES] = turned(index, gq).astype(BF16)
+        return carry
+
+    def key_grads(index, carry):
+        at = chunk_rows(index)
         slot = index * inner + rank
         for p in range(pairs):
-            gq = jnp.transpose(merge_heads(dq_t[p, :, at_q])) * scale
-            gq = gq * cos2 - lane_swap(gq) * sin2
-            gpre[at, p * LANES:(p + 1) * LANES] = gq.astype(BF16)
             for kind in range(2):
                 which = kind * pairs + p
                 total = dkv[slot, which].astype(F32)
@@ -541,12 +611,28 @@
                     total = total + rkv[index, near, which].astype(F32)
                 g = jnp.concatenate([dkvn[index, which], total], axis=0)
                 if kind == 0:
-                    g = g * cos2 - lane_swap(g) * sin2
+                    g = turned(index, g)
                 col = (kind + 1) * head_width + p * LANES
                 gpre[at, col:col + LANES] = g.astype(BF16)
         return carry
 
-    lax.fori_loop(0, groups, pre_grads, 0)
+    def head_grads(kind, base):
+        part = tn(n1[...], gpre[:, kind * head_width:(kind + 1) * head_width])
+        for p in range(pairs):
+            at = base + p * width
+            acc[at:at + width, :] = part[:, p * LANES:(p + 1) * LANES].astype(BF16)
+
+    lax.fori_loop(0, groups, query_grads, 0)
+    query_base = bases[2] + col_tiles * head_width
+    head_grads(0, query_base)
+    tick(2)
+    for index in range(groups):
+        for near in range(1, inner):
+            grad_copy(index, near).wait()
+    lax.fori_loop(0, groups, key_grads, 0)
+    head_grads(1, bases[3])
+    head_grads(2, bases[3] + pairs * width)
+    tick(3)
 
     for piece in range(2):
         lo = piece * half_rows
@@ -555,14 +641,7 @@
         back = back + nt(gpre[lo:lo + half_rows, 2 * head_width:3 * head_width], wh[2])
         head_send(piece, back, 3)
 
-    for kind in range(3):
-        part = tn(n1[...], gpre[:, kind * head_width:(kind + 1) * head_width])
-        for p in range(pairs):
-            at = (kind * pairs + p) * width
-            acc[2, at:at + width, :] = part[:, p * LANES:(p + 1) * LANES].astype(BF16)
-    tick(feed_jobs)
-    head_jobs = [sum_job(2, part) for part in range(3)]
-    tick(head_jobs)
+    tick(0, 1)
 
     def first_back(z, carry):
         gain_sum, shift_sum = carry
@@ -574,13 +653,12 @@
         shift_sum = shift_sum + jnp.sum(upstream, axis=0, keepdims=True)
         return gain_sum, shift_sum
 
-    for copy in y_copies:
-        copy.wait()
+    pass_on(y_spread)
     sums = (zero_row, zero_row)
     for piece in range(2):
         head_copy(piece, 3).wait()
         sums = lax.fori_loop(piece * groups // 2, (piece + 1) * groups // 2, first_back, sums)
-    ig_copies = spread(dyb, ig_out, i_send, i_recv)
+    ig_spread = spread(dyb, ig_out, i_send, i_recv, if_send, if_recv)
     keep_small(1, sums[0])
     keep_small(2, sums[1])
 
@@ -592,35 +670,61 @@
             copy.wait()
             small[...] = small[...] + small_r[bit]
 
-    last = [small_job()]
-    all_jobs = feed_jobs + head_jobs + last
-    for _ in range(2 * bits + 1):
-        tick(all_jobs)
-    small_out[...] = small[...]
-
-    outs = []
+    jobs.append([small_job()])
+    outs = [[], [], [], []]
     for c in range(col_tiles):
         at = slice(c * LANES, (c + 1) * LANES)
-        outs.append((acc.at[0, pl.ds(c * hidden, hidden)], down_out.at[:, at]))
+        outs[0].append((acc.at[pl.ds(bases[0] + c * hidden, hidden)], down_out.at[:, at]))
+        outs[2].append((acc.at[pl.ds(bases[2] + c * head_width, head_width)], wout_out.at[:, at]))
     for c in range(hidden // LANES):
         at = slice(c * LANES, (c + 1) * LANES)
-        outs.append((acc.at[1, pl.ds(c * width, width)], up_out.at[:, at]))
-    for kind in range(3):
-        for p in range(pairs):
-            at = slice(p * LANES, (p + 1) * LANES)
-            outs.append((acc.at[2, pl.ds((kind * pairs + p) * width, width)], heads_out.at[kind, :, at]))
-    for c in range(col_tiles):
-        at = slice(c * LANES, (c + 1) * LANES)
-        outs.append((acc.at[2, pl.ds(out_base + c * head_width, head_width)], wout_out.at[:, at]))
-    copies = [pltpu.make_async_copy(src, dst, out_sem.at[i]) for i, (src, dst) in enumerate(outs)]
-    for copy in copies:
-        copy.start()
+        outs[1].append((acc.at[pl.ds(bases[1] + c * width, width)], up_out.at[:, at]))
+    for p in range(pairs):
+        at = slice(p * LANES, (p + 1) * LANES)
+        outs[2].append((acc.at[pl.ds(query_base + p * width, width)], heads_out.at[0, :, at]))
+        for kind in range(2):
+            outs[3].append(
+                (acc.at[pl.ds(bases[3] + (kind * pairs + p) * width, width)], heads_out.at[kind + 1, :, at])
+            )
+    sem_at = 0
+    copies = []
+
+    def finish(job):
+        nonlocal sem_at
+        for src, dst in outs[job]:
+            copy = pltpu.make_async_copy(src, dst, out_sem.at[sem_at])
+            copy.start()
+            copies.append(copy)
+            sem_at += 1
+
+    order = [0, 1, 2, 3, 4]
+    done = set()
+    for turn in range(2 * bits + 1):
+        tick(*order)
+        if turn == bits:
+            pass_on(ig_spread)
+        for job in range(4):
+            if job not in done and all(steps.gi_frame is None for steps in jobs[job]):
+                finish(job)
+                done.add(job)
+    small_out[...] = small[...]
     for copy in x_copies + c_copies:
         copy.wait_send()
-    for copy in ig_copies:
-        copy.wait()
+    for onward in y_spread[2] + ig_spread[2]:
+        onward.wait()
     for copy in copies:
         copy.wait()
+
+
+def widen(count, *refs):
+    sources, small, targets = refs[:count], refs[count], refs[count + 1:]
+    for source, target in zip(sources, targets):
+        target[...] = source[...].astype(target.dtype)
+    row = 0
+    for target in targets[count:]:
+        for i in range(target.shape[0] // WIDE):
+            target[i * WIDE:(i + 1) * WIDE] = small[row]
+            row += 1
 
 
 def local(
@@ -636,19 +740,8 @@
     chunk = 2 * span
     rows = groups * chunk
     stack = 2 * chunk
-    rank = lax.axis_index("seq") % inner
     bits = int(math.log2(n))
-
-    first = (jnp.arange(groups, dtype=jnp.int32) * inner + rank) * span
-    positions = (first[:, None] + jnp.arange(span, dtype=jnp.int32)[None, :]).astype(F32)
-    lane = jnp.arange(LANES, dtype=jnp.int32)
-    half = HD // 2
-    frequency = jnp.exp((lane % half).astype(F32) * (-math.log(ROTARY_BASE) / half))
-    angles = positions[:, :, None] * frequency[None, None, :]
-    cos_t = jnp.cos(angles)
-    sin_t = jnp.sin(angles) * jnp.where(lane % HD < half, -1.0, 1.0).astype(F32)
-
-    acc_rows = hidden * width // LANES
+    job_rows, bases = job_layout(n, width, head_width, hidden)
     small_rows = (hidden // WIDE + 5 * (width // WIDE) + 7) // 8 * 8
     out_copies = width // LANES + hidden // LANES + 3 * pairs + width // LANES
     anywhere = pl.BlockSpec(memory_space=pl.ANY)
@@ -681,17 +774,21 @@
         pltpu.VMEM((3, rows, width), BF16),
         pltpu.VMEM((rows, width), F32),
         pltpu.VMEM((pairs, LANES, groups * stack), F32),
-        pltpu.VMEM((3, acc_rows, LANES), BF16),
-        pltpu.VMEM((3, acc_rows, LANES), BF16),
+        pltpu.VMEM((bases[-1], LANES), BF16),
+        pltpu.VMEM((bases[-1], LANES), BF16),
         pltpu.VMEM((small_rows, WIDE), F32),
         pltpu.VMEM((bits, small_rows, WIDE), F32),
+        pltpu.VMEM((groups, span, LANES), F32),
+        pltpu.VMEM((groups, span, LANES), F32),
+        pltpu.VMEM((-(-hidden // WIDE // 8) * 8, WIDE), F32),
+        pltpu.VMEM((8, width), F32),
         dma((6,)),
-        dma((groups,)), dma((groups,)), dma((groups,)), dma((groups,)),
+        *[dma((groups,))] * 8,
         dma((groups, inner)), dma((groups, inner)),
         dma((4, 2)), dma((4, 2)),
         dma((groups, inner)), dma((groups, inner)),
-        dma((groups,)), dma((groups,)), dma((groups,)), dma((groups,)),
-        dma((3, 3, 2 * bits)), dma((3, 3, 2 * bits)), pltpu.SemaphoreType.REGULAR((3, 3, bits)),
+        *[dma((groups,))] * 8,
+        dma((4, 3, 2 * bits)), dma((4, 3, 2 * bits)), pltpu.SemaphoreType.REGULAR((4, 3, bits)),
         dma((bits,)), dma((bits,)),
         dma((out_copies,)),
     ]
@@ -707,7 +804,7 @@
     y, ig, down, up, heads, wout, small = pl.pallas_call(
         functools.partial(fused, (n, groups, span, width, head_width, hidden)),
         out_shape=out_shape,
-        in_specs=[anywhere] * 6 + [pl.BlockSpec(memory_space=pltpu.SMEM)] + [vmem] * 8,
+        in_specs=[anywhere] * 6 + [pl.BlockSpec(memory_space=pltpu.SMEM)] + [vmem] * 6,
         out_specs=(anywhere,) * 6 + (vmem,),
         scratch_shapes=scratch,
         compiler_params=pltpu.CompilerParams(
@@ -717,30 +814,28 @@
         layer_input.reshape(groups, chunk, width),
         cotangent.reshape(groups, chunk, width),
         w_heads, w_output, w_up, w_down, block_sizes,
-        mixing_gain[None], mixing_shift[None], feed_gain[None], feed_shift[None],
-        bias_up.reshape(hidden // WIDE, WIDE), bias_down[None], cos_t, sin_t,
+        mixing_gain, mixing_shift, feed_gain, feed_shift, bias_up, bias_down,
     )
-    up_rows = hidden // WIDE
-    per = width // WIDE
-
-    def vector(i):
-        return small[up_rows + i * per:up_rows + (i + 1) * per].reshape(width)
-
     full = (groups, 2, span, width)
-    return (
-        y.reshape(full),
-        ig.astype(F32).reshape(full),
-        heads.astype(F32),
-        wout.astype(F32),
-        up.astype(F32),
-        small[:up_rows].reshape(hidden),
-        down.astype(F32),
-        vector(0),
-        vector(1),
-        vector(2),
-        vector(3),
-        vector(4),
-    )
+    steps = 8
+    sources = (y.reshape(rows, width), ig.reshape(rows, width), heads, wout, up, down)
+    kinds = (BF16,) + (F32,) * 5
+    specs = []
+    for source in sources:
+        shape = source.shape
+        block = shape[:-2] + (shape[-2] // steps, shape[-1])
+        specs.append(pl.BlockSpec(block, lambda i, lead=len(shape) - 2: (0,) * lead + (i, 0)))
+    vector_sizes = (hidden,) + (width,) * 5
+    y, ig, heads, wout, up, down, *vectors = pl.pallas_call(
+        functools.partial(widen, len(sources)),
+        grid=(steps,),
+        out_shape=tuple(jax.ShapeDtypeStruct(a.shape, kind) for a, kind in zip(sources, kinds))
+        + tuple(jax.ShapeDtypeStruct((size,), F32) for size in vector_sizes),
+        in_specs=specs + [pl.BlockSpec(small.shape, lambda i: (0, 0))],
+        out_specs=tuple(specs) + tuple(pl.BlockSpec((size,), lambda i: (0,)) for size in vector_sizes),
+        compiler_params=pltpu.CompilerParams(vmem_limit_bytes=VMEM_BYTES),
+    )(*sources, small)
+    return (y.reshape(full), ig.reshape(full), heads, wout, up, vectors[0], down, *vectors[1:])
 
 
 def solution(mesh):

time: 255 us -> 208 us (0.82)
  Pallas kernels: 229 us -> 207 us
  other arithmetic: 12.9 us -> 0 us
  local copies, waits for them, and re-layouts: 12.1 us -> 0 us
    pallas_call x1, Pallas kernels: 229 us -> 197 us  [local(): pl.pallas_call(functools.partial(fused, (n, groups, span, width, head_wid...]
    pallas_call x0 -> x1, Pallas kernels: none -> 10.5 us  [local(): pl.pallas_call(functools.partial(widen, len(sources)), grid=(steps,), out...]
    convert_element_type x5 -> x0, other arithmetic: 10.4 us -> none  [the longest x1 4.65 us: local(): up.astype(F32)]
    broadcast_in_dim x5 -> x0, local copies, waits for them, and re-layouts: 6.33 us -> none  [the longest x1 1.27 us: local(): feed_gain[None]]
    reshape x7 -> x0, local copies, waits for them, and re-layouts: 4.89 us -> none  [the longest x5 3 us: vector(): return small[up_rows + i * per:up_rows + (i + 1) * per].reshape(width)]
where the time goes in v2:
time: 208 us
  Pallas kernels  207 us (100%)
    pallas_call x1, Pallas kernels, local(): pl.pallas_call(functools.partial(fused, (n, groups, span, width, head_wid...  197 us
    pallas_call x1, Pallas kernels, local(): pl.pallas_call(functools.partial(widen, len(sources)), grid=(steps,), out...  10.5 us

profile of v2, /device:TPU:0, one launch (start us, length us, event | category | flops | bytes accessed | tf_op | source)
XLA Modules:
  0.0 208.1 jit_solution(17420667502668704370)
XLA Ops:
  0.6 196.8 %shard_map.220 = (bf16[4,128,768]{2,1,0:T(8,128)(2,1)}, bf16[4,128,768]{2,1,0:T(8,128)(2,1)}, bf16[1536,768]{1,0:T(8,128)(2,1)}, bf16[768,1536]{1,0:T(8,128)(2,1...) custom-call(bf16[4,128,768]{2,1,0:T(8,128)(2,1)} %bitcast.6, ...), custom_call_target="tpu_custom_call" | custom-call | tf_op jit(solution)/shard_map/pallas_call | solution.py:804
  197.4 10.5 %shard_map.221 = (bf16[512,768]{1,0:T(8,128)(2,1)}, f32[512,768]{1,0:T(8,128)}, f32[3,768,384]{2,1,0:T(8,128)}, f32[384,768]{1,0:T(8,128)}, f32[768,1536]{1,0:T(...) custom-call(bf16[512,768]{1,0:T(8,128)(2,1)} %bitcast.8, ...), custom_call_target="tpu_custom_call" | custom-call | tf_op jit(solution)/shard_map/pallas_call | solution.py:829

commit v3 on v2

--- a/solution.py
+++ b/solution.py
@@ -19,7 +19,15 @@
 F32 = jnp.float32
 BF16 = jnp.bfloat16
 WIDE = 256
-VMEM_BYTES = 66_000_000
+VMEM_BYTES = 66_900_000
+
+
+PART_UNITS = ((7, 7, 4, 7, 7, 4), (7, 7, 4, 7, 7, 4), (7, 7, 4), (7, 7, 4))
+PART_ORDERS = ((0, 1, 2, 1, 0, 3), (0, 1, 2, 1, 0, 3), (0, 1, 2), (0, 1, 2))
+TURNS = ((0, (0, 1, 2)), (0, (3, 4, 5)), (1, (0, 1, 2)), (1, (3, 4, 5)), (2, (0, 1, 2)), (3, (0, 1, 2)), (4, (0,)))
+ROUNDS = {
+    "feed_up": 1, "noisy": 1, "g3": 1, "hq": 1, "hk": 1, "plane": 3, "first_back": 2,
+}
 
 
 def nn(a, b):
@@ -65,10 +73,11 @@
         x_in, c_in, wh_in, wo_in, wu_in, wd_in, blocks,
         gain_one_in, shift_one_in, gain_two_in, shift_two_in, bias_up_in, bias_down_in,
         y_out, ig_out, down_out, up_out, heads_out, wout_out, small_out,
-        wh, wo, wu, wd, xb, dyb, n1, n2, qs, dos, kv, kvn, dkv, rkv, dkvn, lses, deltas, att, att_f,
-        middle, hid, gpre, send_h, recv_h, grad_mid, dq_t,
-        acc, arr, small, small_r, cos_t, sin_t, bias_rows, vectors,
-        w_sem, x_send, x_recv, c_send, c_recv, xf_send, xf_recv, cf_send, cf_recv, kv_send, kv_recv, h_send, h_recv, g_send, g_recv,
+        wh, wo, wu, wd, xb, dyb, n1, n2, nc, qs, dos, kv, kvn, lses, deltas, att,
+        middle, hid, gpre, send_h, recv_h, grad_mid, dq_t, core_part, plane_part, clean_sum,
+        acc, arr, small, small_r, cos_a, sin_a, cos_b, sin_b, bias_rows, vectors,
+        w_sem, xc_send, xc_recv, xn_send, xn_recv, c_send, c_recv, xcf_send, xcf_recv, xnf_send, xnf_recv, cf_send, cf_recv,
+        kv_send, kv_recv, loc_sem, ncf_send, ncf_recv, h_send, h_recv, g_send, g_recv, k_send, k_recv,
         y_send, y_recv, i_send, i_recv, yf_send, yf_recv, if_send, if_recv, ar_send, ar_recv, ar_free, sm_send, sm_recv, out_sem,
     ) = refs
     inner = n // groups
@@ -125,26 +134,63 @@
     weight_copies[0].start()
     pl.semaphore_wait(barrier, groups + inner - 1)
 
-    x_copies, c_copies, x_passes, c_passes = [], [], [], []
-    share = pl.ds(pl.multiple_of(core * span, span), span)
+    clean_copies, noisy_copies, c_copies = [], [], []
+    clean_passes, noisy_passes, c_passes = [], [], []
+    share_rows = span // 2
+    share = pl.ds(pl.multiple_of(core * share_rows, share_rows), share_rows)
+    other_share = pl.ds(pl.multiple_of((1 - core) * share_rows, share_rows), share_rows)
     for step in range(1, groups):
         to = group_peer(step)
         source = group_peer(groups - step)
         where = peer(to * inner + rank)
-        x_copies.append(
-            remote(x_in.at[to, share], xb.at[group, share], x_send.at[step], x_recv.at[step], where)
+        clean_copies.append(
+            remote(x_in.at[to, 1, share], xb.at[group, 1, share], xc_send.at[step], xc_recv.at[step], where)
+        )
+        noisy_copies.append(
+            remote(x_in.at[to, 0, share], xb.at[group, 0, share], xn_send.at[step], xn_recv.at[step], where)
         )
         c_copies.append(
-            remote(c_in.at[to, share], dyb.at[group, share], c_send.at[step], c_recv.at[step], where)
+            remote(c_in.at[to, :, share], dyb.at[group, :, share], c_send.at[step], c_recv.at[step], where)
         )
-        x_passes.append(
-            remote(xb.at[source, share], xb.at[source, share], xf_send.at[step], xf_recv.at[step], sibling)
+        clean_passes.append(
+            remote(xb.at[source, 1, share], xb.at[source, 1, share], xcf_send.at[step], xcf_recv.at[step], sibling)
+        )
+        noisy_passes.append(
+            remote(xb.at[source, 0, share], xb.at[source, 0, share], xnf_send.at[step], xnf_recv.at[step], sibling)
         )
         c_passes.append(
-            remote(dyb.at[source, share], dyb.at[source, share], cf_send.at[step], cf_recv.at[step], sibling)
+            remote(dyb.at[source, :, share], dyb.at[source, :, share], cf_send.at[step], cf_recv.at[step], sibling)
         )
-    for copy in x_copies:
+    for copy in clean_copies + noisy_copies:
         copy.start()
+
+    def plane_copy(index, near):
+        slot = index * inner + rank
+        return remote(
+            xb.at[index, 1, share], nc.at[slot, share], kv_send.at[index, near], kv_recv.at[index, near],
+            peer(group * inner + plane_peer(near)),
+        )
+
+    def own_clean(index):
+        return pltpu.make_async_copy(xb.at[index, 1, share], nc.at[index * inner + rank, share], loc_sem.at[index])
+
+    def plane_send(index):
+        for near in range(1, inner):
+            plane_copy(index, near).start()
+        own_clean(index).start()
+
+    def plane_pass(index):
+        at = pl.ds(index * inner, inner)
+        return remote(nc.at[at, share], nc.at[at, share], ncf_send.at[index], ncf_recv.at[index], sibling)
+
+    def plane_done(index):
+        own_clean(index).wait()
+        for near in range(1, inner):
+            plane_copy(index, near).wait()
+        plane_pass(index).start()
+
+    own_x.wait()
+    plane_send(group)
     for copy in weight_copies[1:]:
         copy.start()
     own_c.start()
@@ -171,70 +217,86 @@
     lane = lax.broadcasted_iota(jnp.int32, (1, LANES), 1)
     frequency = jnp.exp((lane % half_head).astype(F32) * (-math.log(ROTARY_BASE) / half_head))
     sign = jnp.where(lane % HD < half_head, -1.0, 1.0)
-    for index in range(groups):
-        start = (index * inner + rank) * span
-        position = lax.broadcasted_iota(jnp.int32, (span, LANES), 0) + start
-        angle = position.astype(F32) * frequency
-        cos_t[index] = jnp.cos(angle)
-        sin_t[index] = jnp.sin(angle) * sign
-
-
-    def project(index):
-        x = xb[index].astype(F32)
+    start = lax.broadcasted_iota(jnp.int32, (n, LANES), 0) * span
+    angle = start.astype(F32) * frequency
+    cos_a[...] = jnp.cos(angle)
+    sin_a[...] = jnp.sin(angle) * sign
+    angle = lax.broadcasted_iota(jnp.int32, (span, LANES), 0).astype(F32) * frequency
+    cos_b[...] = jnp.cos(angle)
+    sin_b[...] = jnp.sin(angle) * sign
+
+    def tables(slot):
+        cos = cos_a[pl.ds(slot, 1), :]
+        sin = sin_a[pl.ds(slot, 1), :]
+        return cos * cos_b[...] - sin * sin_b[...], sin * cos_b[...] + cos * sin_b[...]
+
+    def turn(value, table):
+        return value * table[0] + lane_swap(value) * table[1]
+
+    def turn_back(value, table):
+        return value * table[0] - lane_swap(value) * table[1]
+
+    def twice(table):
+        return tuple(jnp.concatenate([part, part], axis=0) for part in table)
+
+    def many(first, count):
+        parts = [tables(first + i) for i in range(count)]
+        return tuple(jnp.concatenate([part[i] for part in parts], axis=0) for i in range(2))
+
+    weight_copies[0].wait()
+    for step in range(1, groups):
+        clean_copies[step - 1].wait_recv()
+        plane_send(group_peer(groups - step))
+        clean_passes[step - 1].start()
+    for step in range(1, groups):
+        noisy_copies[step - 1].wait_recv()
+        noisy_passes[step - 1].start()
+    for copy in c_copies:
+        copy.start()
+    plane_done(group)
+    for copy in clean_passes + noisy_passes:
+        copy.wait()
+
+    def first_norm(z, carry):
+        hat, _ = norm_stats(xb[z].reshape(chunk, width).astype(F32))
+        n1[z] = (hat * gain_one[...] + shift_one[...]).astype(BF16).reshape(2, span, width)
+        return carry
+
+    lax.fori_loop(0, groups, first_norm, 0)
+
+    def queries(z, carry):
+        out = nn(n1[z].reshape(chunk, width), wh[0])
+        table = twice(tables(z * inner + rank))
+        at_q = pl.ds(pl.multiple_of(z * stack, stack), stack)
+        for p in range(pairs):
+            low = (turn(out[:, p * LANES:(p + 1) * LANES], table) * scale).astype(BF16)
+            qs[p, at_q, :] = stack_heads(low)
+        return carry
+
+    lax.fori_loop(0, groups, queries, 0)
+    noisy_rows = n1[:, 0].reshape(groups * span, width)
+    for kind in range(2):
+        out = nn(noisy_rows, wh[kind + 1])
+        for z in range(groups):
+            table = tables(z * inner + rank)
+            for p in range(pairs):
+                part = out[z * span:(z + 1) * span, p * LANES:(p + 1) * LANES]
+                kvn[z, kind * pairs + p] = (part if kind else turn(part, table)).astype(BF16)
+    for step in range(1, groups):
+        plane_done(group_peer(groups - step))
+
+    def clean_rows(first):
+        x = nc[first:first + key_ranks].reshape(key_ranks * span, width).astype(F32)
         hat, _ = norm_stats(x)
         normed = (hat * gain_one[...] + shift_one[...]).astype(BF16)
-        n1[pl.ds(pl.multiple_of(index * chunk, chunk), chunk), :] = normed
-        slot = index * inner + rank
-        cos = cos_t[index]
-        sin = sin_t[index]
-        cos2 = jnp.concatenate([cos, cos], axis=0)
-        sin2 = jnp.concatenate([sin, sin], axis=0)
-        at_q = pl.ds(pl.multiple_of(index * stack, stack), stack)
-        for kind in range(3):
-            out = nn(normed, wh[kind])
+        nc[first:first + key_ranks] = normed.reshape(key_ranks, span, width)
+        table = many(first, key_ranks)
+        for kind in range(2):
+            out = nn(normed, wh[kind + 1])
             for p in range(pairs):
                 part = out[:, p * LANES:(p + 1) * LANES]
-                if kind < 2:
-                    part = part * cos2 + lane_swap(part) * sin2
-                if kind == 0:
-                    part = part * scale
-                low = part.astype(BF16)
-                if kind == 0:
-                    qs[p, at_q, :] = stack_heads(low)
-                else:
-                    where = (kind - 1) * pairs + p
-                    kvn[index, where] = low[:span]
-                    kv[slot, where] = low[span:]
-
-    for step in range(groups):
-        index = group_peer(groups - step) if step else group
-        if step == 0:
-            own_x.wait()
-            weight_copies[0].wait()
-        else:
-            x_passes[step - 1].wait()
-        project(index)
-        if step == 0:
-            for copy, onward in zip(x_copies, x_passes):
-                copy.wait_recv()
-                onward.start()
-            for copy in c_copies:
-                copy.start()
-        slot = index * inner + rank
-        for near in range(1, inner):
-            copy = remote(
-                kv.at[slot], kv.at[slot], kv_send.at[index, near], kv_recv.at[index, near],
-                peer(group * inner + plane_peer(near)),
-            )
-            copy.start()
-
-    def kv_wait(index):
-        for near in range(1, inner):
-            source = index * inner + plane_peer(inner - near)
-            remote(
-                kv.at[source], kv.at[source], kv_send.at[index, near], kv_recv.at[index, near],
-                peer(group * inner + plane_peer(near)),
-            ).wait()
+                low = (part if kind else turn(part, table)).astype(BF16)
+                kv[first:first + key_ranks, kind * pairs + p] = low.reshape(key_ranks, span, LANES)
 
     def clean_mask(index, first_rank, count, shape):
         key = lax.broadcasted_iota(jnp.int32, shape, 0) + first_rank * span
@@ -244,35 +306,27 @@
         key = lax.broadcasted_iota(jnp.int32, shape, 0) & (-size_b)
         return (key == start_q) & jnp.logical_not(clean_q)
 
-    own_c.wait()
-    for copy, onward in zip(c_copies, c_passes):
-        copy.wait_recv()
-        onward.start()
-    weight_copies[2].wait()
-    weight_copies[3].wait()
-    for copy in c_passes:
-        copy.wait()
-
     def feed_back(i, carry):
         cols = pl.ds(pl.multiple_of(i * WIDE, WIDE), WIDE)
         gpre[:, cols] = nt(dyb[...].reshape(rows, width), wd[cols, :]).astype(BF16)
         return carry
 
-    lax.fori_loop(0, up_bias_rows, feed_back, 0)
-
     def head_send(piece, value, which):
-        send_h[which % 3, piece * half_rows:(piece + 1) * half_rows, :] = value.astype(BF16)
-        copy = head_copy(piece, which)
-        copy.start()
+        at = slice(piece * groups // 2, (piece + 1) * groups // 2)
+        send_h[which % 2, at] = value.astype(BF16).reshape(groups // 2, 2, span, width)
+        if which != 2:
+            head_copy(piece, which).start()
 
     def head_copy(piece, which):
-        at = pl.ds(piece * half_rows, half_rows)
+        at = pl.ds(piece * groups // 2, groups // 2)
         return remote(
-            send_h.at[which % 3, at], recv_h.at[which % 3, at], h_send.at[which, piece], h_recv.at[which, piece], sibling
+            send_h.at[which % 2, at], recv_h.at[which % 2, at], h_send.at[which, piece], h_recv.at[which, piece], sibling
         )
 
     for index in range(groups):
-        kv_wait(index)
+        plane_pass(index).wait()
+        for block in range(key_blocks):
+            clean_rows(index * inner + block * key_ranks)
 
         def attend(p, carry, index=index):
             q = qs[p, index * stack:(index + 1) * stack, :]
@@ -298,8 +352,9 @@
                 vals = kv[g * inner:(g + 1) * inner, pairs + p].reshape(inner * span, LANES)
                 out = out + tn(vals, e.astype(BF16))
             lses[p, :, index * stack:(index + 1) * stack] = top + jnp.log(total)
-            rows_out = jnp.transpose(merge_heads(out / total))
-            att_f[p, index * chunk:(index + 1) * chunk, :] = rows_out
+            merged = merge_heads(out / total)
+            rows_out = jnp.transpose(merged)
+            dq_t[p, :, index * stack:index * stack + chunk] = merged
             at = pl.ds(pl.multiple_of(p * LANES, LANES), LANES)
             att[index * chunk:(index + 1) * chunk, at] = rows_out.astype(BF16)
             return carry
@@ -310,13 +365,25 @@
         if index % (groups // 2) == groups // 2 - 1:
             piece = index // (groups // 2)
             head_send(piece, nn(att[piece * half_rows:(piece + 1) * half_rows, :], wo[...]), 0)
+        if index == groups // 2:
+            own_c.wait()
+            for copy, onward in zip(c_copies, c_passes):
+                copy.wait_recv()
+                onward.start()
+
+    weight_copies[2].wait()
+    weight_copies[3].wait()
+    for copy in c_passes:
+        copy.wait()
+    lax.fori_loop(0, up_bias_rows, feed_back, 0)
 
     def chunk_rows(z):
         return pl.ds(pl.multiple_of(z * chunk, chunk), chunk)
 
     def second_norm(z, carry):
         at = chunk_rows(z)
-        mid = xb[z].astype(F32) + (send_h[0, at, :].astype(F32) + recv_h[0, at, :].astype(F32))
+        mixed = send_h[0, z].astype(F32) + recv_h[0, z].astype(F32)
+        mid = (xb[z].astype(F32) + mixed).reshape(chunk, width)
         middle[at, :] = mid
         hat, _ = norm_stats(mid)
         n2[at, :] = (hat * gain_two[...] + shift_two[...]).astype(BF16)
@@ -361,10 +428,15 @@
         return carry
 
     low_bits = int(math.log2(inner))
+    plane_bits, group_bits = list(range(low_bits)), list(range(low_bits, bits))
+    turned_bits = plane_bits[1::-1] + plane_bits[2:]
     orders = [
-        list(range(bits)),
-        [1, 0] + list(range(2, bits)),
-        list(range(low_bits, bits)) + list(range(low_bits)),
+        plane_bits + group_bits,
+        turned_bits + group_bits,
+        group_bits + plane_bits,
+        group_bits + turned_bits,
+        turned_bits[:1] + group_bits + turned_bits[1:],
+        plane_bits[:1] + group_bits + plane_bits[1:],
     ]
 
     def bit_of(bit):
@@ -374,12 +446,14 @@
         return peer(me + (1 - 2 * bit_of(bit)) * (1 << bit))
 
     def sum_steps(job, part):
-        seg = job_rows[job] // n
-        first = max(16, int(seg * 0.4 / 16 + 0.5) * 16)
-        sizes = [first, first, seg - 2 * first]
-        base = bases[job] + n * sum(sizes[:part])
-        s = sizes[part]
-        order = orders[part]
+        weights = PART_UNITS[job]
+        units = job_rows[job] // n // 16
+        edges = [(2 * sum(weights[:i]) * units + sum(weights)) // (2 * sum(weights)) for i in range(len(weights) + 1)]
+        base = bases[job] + n * 16 * edges[part]
+        s = 16 * (edges[part + 1] - edges[part])
+        order = orders[PART_ORDERS[job][part]]
+        if s == 0:
+            return
         lo = 0
         size = n
 
@@ -419,24 +493,78 @@
             lo = lo - bit_of(bit) * size
             size = size * 2
 
-    jobs = [[sum_steps(job, part) for part in range(3)] for job in range(len(job_rows))]
-
-    def tick(*which):
-        for job in which:
-            for steps in jobs[job]:
-                next(steps, None)
+    jobs = [[sum_steps(job, part) for part in range(len(PART_UNITS[job]))] for job in range(len(job_rows))]
+    query_base = bases[2] + col_tiles * head_width
+    copies = []
+    finished = set()
+    outs = [[], [], [], []]
+    for c in range(col_tiles):
+        at = slice(c * LANES, (c + 1) * LANES)
+        outs[0].append((acc.at[pl.ds(bases[0] + c * hidden, hidden)], down_out.at[:, at]))
+        outs[2].append((acc.at[pl.ds(bases[2] + c * head_width, head_width)], wout_out.at[:, at]))
+    for c in range(hidden // LANES):
+        at = slice(c * LANES, (c + 1) * LANES)
+        outs[1].append((acc.at[pl.ds(bases[1] + c * width, width)], up_out.at[:, at]))
+    for p in range(pairs):
+        at = slice(p * LANES, (p + 1) * LANES)
+        outs[2].append((acc.at[pl.ds(query_base + p * width, width)], heads_out.at[0, :, at]))
+        for kind in range(2):
+            outs[3].append(
+                (acc.at[pl.ds(bases[3] + (kind * pairs + p) * width, width)], heads_out.at[kind + 1, :, at])
+            )
+    sem_at = 0
+
+    def finish(job):
+        nonlocal sem_at
+        for src, dst in outs[job]:
+            copy = pltpu.make_async_copy(src, dst, out_sem.at[sem_at])
+            copy.start()
+            copies.append(copy)
+            sem_at += 1
+
+
+    def advance(job, part):
+        next(jobs[job][part], None)
+        if job < 4 and job not in finished and all(steps.gi_frame is None for steps in jobs[job]):
+            finish(job)
+            finished.add(job)
+
+
+    released = set()
+    running, waiting = [], list(TURNS)
+
+    def take_round():
+        for job, parts in running:
+            for part in parts:
+                advance(job, part)
+        if waiting and waiting[0][0] in released:
+            job, parts = waiting.pop(0)
+            running.append((job, parts))
+            for part in parts:
+                advance(job, part)
+
+    def point(name):
+        for _ in range(ROUNDS.get(name, 0)):
+            take_round()
+
+    def begin(job):
+        released.add(job)
 
     lax.fori_loop(0, up_bias_rows, feed, 0)
-    tick(0)
+    begin(0)
+    take_round()
     lax.fori_loop(0, up_bias_rows, feed_up, 0)
-    tick(1)
+    begin(1)
+    point("feed_up")
 
     for piece in range(2):
         lo = piece * half_rows
         head_send(piece, nt(gpre[lo:lo + half_rows, :], wu[...]), 1)
+    point("back2")
     for piece in range(2):
         lo = piece * half_rows
         head_send(piece, nn(hid[lo:lo + half_rows, :], wd[...]), 2)
+    point("fed")
 
     def norm_back(hat, inv, gain, upstream):
         scaled = upstream * gain
@@ -447,9 +575,9 @@
     def second_back(z, carry):
         gain_sum, shift_sum, bias_sum = carry
         at = chunk_rows(z)
-        upstream = send_h[1, at, :].astype(F32) + recv_h[1, at, :].astype(F32)
+        upstream = (send_h[1, z].astype(F32) + recv_h[1, z].astype(F32)).reshape(chunk, width)
         hat, inv = norm_stats(middle[at, :])
-        dy = dyb[z].astype(F32)
+        dy = dyb[z].astype(F32).reshape(chunk, width)
         total = dy + norm_back(hat, inv, gain_two[...], upstream)
         grad_mid[at, :] = total
         n2[at, :] = total.astype(BF16)
@@ -472,6 +600,9 @@
     keep_small(0, sums[2])
     keep_small(3, sums[0])
     keep_small(4, sums[1])
+    for piece in range(2):
+        head_copy(piece, 2).start()
+    point("second_back")
 
     def attended_back(z, carry):
         at = chunk_rows(z)
@@ -480,19 +611,21 @@
         for p in range(pairs):
             low = back[:, p * LANES:(p + 1) * LANES].astype(BF16)
             dos[p, at_q, :] = stack_heads(low)
-            prod = jnp.transpose(low.astype(F32) * att_f[p, at, :])
+            at_o = pl.ds(pl.multiple_of(z * stack, stack), chunk)
+            prod = jnp.transpose(low.astype(F32)) * dq_t[p, :, at_o]
             d0 = jnp.sum(prod[:HD], axis=0, keepdims=True)
             d1 = jnp.sum(prod[HD:], axis=0, keepdims=True)
             deltas[p, :, at_q] = jnp.concatenate([d0, d1], axis=1)
         return carry
 
     lax.fori_loop(0, groups, attended_back, 0)
-    tick(0, 1)
+    point("att_back")
 
     wout = tn(att[...], n2[...])
     for c in range(col_tiles):
         at = bases[2] + c * head_width
         acc[at:at + head_width, :] = wout[:, c * LANES:(c + 1) * LANES].astype(BF16)
+    point("wout")
 
     def noisy_back(p, carry):
         for index in range(groups):
@@ -505,19 +638,16 @@
             e = jnp.exp(s - lses[p, :, at])
             dp = nt(kvn[index, pairs + p], do)
             ds = (e * (dp - deltas[p, :, at])).astype(BF16)
-            dkvn[index, pairs + p] = nn(e.astype(BF16), do)
-            dkvn[index, p] = nn(ds, q)
+            at_n = slice(index * span, (index + 1) * span)
+            cols = pl.multiple_of(head_width + p * LANES, LANES)
+            gpre[at_n, pl.ds(cols, LANES)] = turn_back(nn(ds, q), tables(index * inner + rank)).astype(BF16)
+            cols = pl.multiple_of(2 * head_width + p * LANES, LANES)
+            gpre[at_n, pl.ds(cols, LANES)] = nn(e.astype(BF16), do).astype(BF16)
             dq_t[p, :, at] = tn(keys, ds)
         return carry
 
     lax.fori_loop(0, pairs, noisy_back, 0)
-
-    def grad_copy(index, near):
-        dest = plane_peer(near)
-        return remote(
-            dkv.at[index * inner + dest], rkv.at[index, near - 1], g_send.at[index, near], g_recv.at[index, near],
-            peer(group * inner + dest),
-        )
+    point("noisy")
 
     for index in range(groups):
         for block in range(key_blocks):
@@ -540,27 +670,82 @@
                 dp = nt(vals, do)
                 ds = (e * (dp - deltas[p, :, at])).astype(BF16)
                 dv = nn(e.astype(BF16), do).astype(BF16)
-                dk = nn(ds, q).astype(BF16)
-                dkv[first:first + key_ranks, p] = dk.reshape(key_ranks, span, LANES)
-                dkv[first:first + key_ranks, pairs + p] = dv.reshape(key_ranks, span, LANES)
+                dk = turn_back(nn(ds, q), many(first, key_ranks)).astype(BF16)
                 dq_t[p, :, at] += tn(keys, ds)
+                kv[first:first + key_ranks, p] = dk.reshape(key_ranks, span, LANES)
+                kv[first:first + key_ranks, pairs + p] = dv.reshape(key_ranks, span, LANES)
                 return carry
 
-            lax.fori_loop(0, pairs, clean_back, 0)
-        for near in range(1, inner):
-            grad_copy(index, near).start()
-        tick(0, 1)
+            if index < groups // 2:
+                for p in range(pairs):
+                    clean_back(p, 0)
+                    point(f"g{index}p{p}")
+            else:
+                lax.fori_loop(0, pairs, clean_back, 0)
+                point(f"g{index}")
+
+    def query_grads(index, carry):
+        at = chunk_rows(index)
+        at_q = pl.ds(pl.multiple_of(index * stack, stack), stack)
+        table = twice(tables(index * inner + rank))
+        for p in range(pairs):
+            gq = jnp.transpose(merge_heads(dq_t[p, :, at_q])) * scale
+            gpre[at, p * LANES:(p + 1) * LANES] = turn_back(gq, table).astype(BF16)
+        return carry
+
+    def keep_heads(part, base):
+        for p in range(part.shape[1] // LANES):
+            at = base + p * width
+            acc[at:at + width, :] = part[:, p * LANES:(p + 1) * LANES].astype(BF16)
+
+    lax.fori_loop(0, groups, query_grads, 0)
+    point("qg")
+    keep_heads(tn(n1[...].reshape(rows, width), gpre[:, :head_width]), query_base)
+    begin(2)
+    point("hq")
+    sweep = min(n, 16)
+    many_rows = sweep * span
+    widths = 2 * pairs if n <= 16 else pairs
+    for lead in range(0, 2 * pairs, widths):
+        at = head_width + lead * LANES
+        part = tn(n1[:, 0].reshape(groups * span, width), gpre[:groups * span, at:at + widths * LANES])
+        for first in range(0, n, sweep):
+            gates = jnp.concatenate(
+                [kv[first:first + sweep, lead + i].reshape(many_rows, LANES) for i in range(widths)], axis=1
+            )
+            part = part + tn(nc[first:first + sweep].reshape(many_rows, width), gates)
+        keep_heads(part, bases[3] + lead * width)
+    begin(3)
+    point("hk")
+
+    def clean_input(block, carry):
+        at = pl.ds(block * key_ranks, key_ranks)
+        total = None
+        for kind in range(2):
+            gates = jnp.concatenate(
+                [kv[at, kind * pairs + p].reshape(key_ranks * span, LANES) for p in range(pairs)], axis=1
+            )
+            back = nt(gates, wh[kind + 1])
+            total = back if total is None else total + back
+        nc[at] = total.astype(BF16).reshape(key_ranks, span, width)
+        return carry
+
+    lax.fori_loop(0, n // key_ranks, clean_input, 0)
+    core_copy = remote(nc.at[:, other_share], core_part, k_send.at[0], k_recv.at[0], sibling)
+    core_copy.start()
+    point("clean_in")
 
     def feed_out(z, carry):
         at = chunk_rows(z)
-        fed = send_h[2, at, :].astype(F32) + recv_h[2, at, :].astype(F32)
-        dyb[z] = (middle[at, :] + fed + bias_down[...]).astype(BF16)
+        fed = (send_h[0, z].astype(F32) + recv_h[0, z].astype(F32)).reshape(chunk, width)
+        dyb[z] = (middle[at, :] + fed + bias_down[...]).astype(BF16).reshape(2, span, width)
         return carry
 
     for piece in range(2):
         head_copy(piece, 2).wait()
     lax.fori_loop(0, groups, feed_out, 0)
 
+    point("feed_out")
     def spread(buf, out, ssem, rsem, psend, precv):
         copies, passes = [], []
         own = pltpu.make_async_copy(buf.at[group], out.at[group], ssem.at[0])
@@ -569,9 +754,9 @@
             to = group_peer(step)
             source = group_peer(groups - step)
             copies.append(
-                remote(buf.at[to, share], out.at[group, share], ssem.at[step], rsem.at[step], peer(to * inner + rank))
+                remote(buf.at[to, :, share], out.at[group, :, share], ssem.at[step], rsem.at[step], peer(to * inner + rank))
             )
-            passes.append(remote(out.at[source, share], out.at[source, share], psend.at[step], precv.at[step], sibling))
+            passes.append(remote(out.at[source, :, share], out.at[source, :, share], psend.at[step], precv.at[step], sibling))
         for copy in copies:
             copy.start()
         return own, copies, passes
@@ -585,70 +770,65 @@
 
     y_spread = spread(dyb, y_out, y_send, y_recv, yf_send, yf_recv)
 
-    def turned(index, grad):
-        cos = cos_t[index]
-        sin = sin_t[index]
-        cos2 = jnp.concatenate([cos, cos], axis=0)
-        sin2 = jnp.concatenate([sin, sin], axis=0)
-        return grad * cos2 - lane_swap(grad) * sin2
-
-    def query_grads(index, carry):
-        at = chunk_rows(index)
-        at_q = pl.ds(pl.multiple_of(index * stack, stack), stack)
-        for p in range(pairs):
-            gq = jnp.transpose(merge_heads(dq_t[p, :, at_q])) * scale
-            gpre[at, p * LANES:(p + 1) * LANES] = turned(index, gq).astype(BF16)
-        return carry
-
-    def key_grads(index, carry):
-        at = chunk_rows(index)
-        slot = index * inner + rank
-        for p in range(pairs):
-            for kind in range(2):
-                which = kind * pairs + p
-                total = dkv[slot, which].astype(F32)
-                for near in range(inner - 1):
-                    total = total + rkv[index, near, which].astype(F32)
-                g = jnp.concatenate([dkvn[index, which], total], axis=0)
-                if kind == 0:
-                    g = turned(index, g)
-                col = (kind + 1) * head_width + p * LANES
-                gpre[at, col:col + LANES] = g.astype(BF16)
-        return carry
-
-    def head_grads(kind, base):
-        part = tn(n1[...], gpre[:, kind * head_width:(kind + 1) * head_width])
-        for p in range(pairs):
-            at = base + p * width
-            acc[at:at + width, :] = part[:, p * LANES:(p + 1) * LANES].astype(BF16)
-
-    lax.fori_loop(0, groups, query_grads, 0)
-    query_base = bases[2] + col_tiles * head_width
-    head_grads(0, query_base)
-    tick(2)
+    for piece in range(2):
+        lo = piece * half_rows
+        back = nt(gpre[lo:lo + half_rows, :head_width], wh[0]).reshape(groups // 2, 2, span, width)
+        lo = lo // 2
+        extra = nt(gpre[lo:lo + half_rows // 2, head_width:2 * head_width], wh[1])
+        extra = extra + nt(gpre[lo:lo + half_rows // 2, 2 * head_width:3 * head_width], wh[2])
+        extra = extra.reshape(groups // 2, span, width)
+        at = slice(piece * groups // 2, (piece + 1) * groups // 2)
+        send_h[1, at, 0] = (back[:, 0] + extra).astype(BF16)
+        send_h[1, at, 1] = back[:, 1].astype(BF16)
+        head_copy(piece, 3).start()
+    point("back1")
+    core_copy.wait()
+
+    def core_add(slot, carry):
+        nc[slot, share] = (nc[slot, share].astype(F32) + core_part[slot].astype(F32)).astype(BF16)
+        return carry
+
+    lax.fori_loop(0, n, core_add, 0)
+    point("core_add")
+
+    def part_copy(index, near):
+        dest = plane_peer(near)
+        return remote(
+            nc.at[index * inner + dest, share], plane_part.at[index, near - 1], g_send.at[index, near],
+            g_recv.at[index, near], peer(group * inner + dest),
+        )
+
     for index in range(groups):
         for near in range(1, inner):
-            grad_copy(index, near).wait()
-    lax.fori_loop(0, groups, key_grads, 0)
-    head_grads(1, bases[3])
-    head_grads(2, bases[3] + pairs * width)
-    tick(3)
-
-    for piece in range(2):
-        lo = piece * half_rows
-        back = nt(gpre[lo:lo + half_rows, :head_width], wh[0])
-        back = back + nt(gpre[lo:lo + half_rows, head_width:2 * head_width], wh[1])
-        back = back + nt(gpre[lo:lo + half_rows, 2 * head_width:3 * head_width], wh[2])
-        head_send(piece, back, 3)
-
-    tick(0, 1)
+            part_copy(index, near).start()
+    point("plane")
+    for index in range(groups):
+        for near in range(1, inner):
+            part_copy(index, near).wait()
+
+    def clean_add(index, carry):
+        total = nc[index * inner + rank, share].astype(F32)
+        for near in range(inner - 1):
+            total = total + plane_part[index, near].astype(F32)
+        clean_sum[index, share] = total.astype(BF16)
+        return carry
+
+    lax.fori_loop(0, groups, clean_add, 0)
+    sum_copy = remote(clean_sum.at[:, share], clean_sum.at[:, share], k_send.at[1], k_recv.at[1], sibling)
+    sum_copy.start()
+    point("clean_add")
+    sum_copy.wait()
+    point("sum")
 
     def first_back(z, carry):
         gain_sum, shift_sum = carry
         at = chunk_rows(z)
-        upstream = send_h[0, at, :].astype(F32) + recv_h[0, at, :].astype(F32)
-        hat, inv = norm_stats(xb[z].astype(F32))
-        dyb[z] = (grad_mid[at, :] + norm_back(hat, inv, gain_one[...], upstream)).astype(BF16)
+        clean = clean_sum[z].astype(F32)
+        upstream = (send_h[1, z].astype(F32) + recv_h[1, z].astype(F32)).reshape(chunk, width)
+        upstream = upstream + jnp.concatenate([jnp.zeros_like(clean), clean], axis=0)
+        hat, inv = norm_stats(xb[z].astype(F32).reshape(chunk, width))
+        total = grad_mid[at, :] + norm_back(hat, inv, gain_one[...], upstream)
+        dyb[z] = total.astype(BF16).reshape(2, span, width)
         gain_sum = gain_sum + jnp.sum(upstream * hat, axis=0, keepdims=True)
         shift_sum = shift_sum + jnp.sum(upstream, axis=0, keepdims=True)
         return gain_sum, shift_sum
@@ -671,44 +851,14 @@
             small[...] = small[...] + small_r[bit]
 
     jobs.append([small_job()])
-    outs = [[], [], [], []]
-    for c in range(col_tiles):
-        at = slice(c * LANES, (c + 1) * LANES)
-        outs[0].append((acc.at[pl.ds(bases[0] + c * hidden, hidden)], down_out.at[:, at]))
-        outs[2].append((acc.at[pl.ds(bases[2] + c * head_width, head_width)], wout_out.at[:, at]))
-    for c in range(hidden // LANES):
-        at = slice(c * LANES, (c + 1) * LANES)
-        outs[1].append((acc.at[pl.ds(bases[1] + c * width, width)], up_out.at[:, at]))
-    for p in range(pairs):
-        at = slice(p * LANES, (p + 1) * LANES)
-        outs[2].append((acc.at[pl.ds(query_base + p * width, width)], heads_out.at[0, :, at]))
-        for kind in range(2):
-            outs[3].append(
-                (acc.at[pl.ds(bases[3] + (kind * pairs + p) * width, width)], heads_out.at[kind + 1, :, at])
-            )
-    sem_at = 0
-    copies = []
-
-    def finish(job):
-        nonlocal sem_at
-        for src, dst in outs[job]:
-            copy = pltpu.make_async_copy(src, dst, out_sem.at[sem_at])
-            copy.start()
-            copies.append(copy)
-            sem_at += 1
-
-    order = [0, 1, 2, 3, 4]
-    done = set()
-    for turn in range(2 * bits + 1):
-        tick(*order)
-        if turn == bits:
-            pass_on(ig_spread)
-        for job in range(4):
-            if job not in done and all(steps.gi_frame is None for steps in jobs[job]):
-                finish(job)
-                done.add(job)
+    begin(4)
+    point("first_back")
+    pass_on(ig_spread)
+    point("ig")
+    while any(steps.gi_frame is not None for job in jobs for steps in job):
+        take_round()
     small_out[...] = small[...]
-    for copy in x_copies + c_copies:
+    for copy in clean_copies + noisy_copies + c_copies:
         copy.wait_send()
     for onward in y_spread[2] + ig_spread[2]:
         onward.wait()
@@ -747,54 +897,57 @@
     anywhere = pl.BlockSpec(memory_space=pl.ANY)
     vmem = pl.BlockSpec(memory_space=pltpu.VMEM)
     dma = pltpu.SemaphoreType.DMA
+    own = pltpu.VMEM((groups, 2, span, width), BF16)
     scratch = [
         pltpu.VMEM((3, width, head_width), BF16),
         pltpu.VMEM((head_width, width), BF16),
         pltpu.VMEM((width, hidden), BF16),
         pltpu.VMEM((hidden, width), BF16),
-        pltpu.VMEM((groups, chunk, width), BF16),
-        pltpu.VMEM((groups, chunk, width), BF16),
+        own,
+        own,
+        own,
         pltpu.VMEM((rows, width), BF16),
-        pltpu.VMEM((rows, width), BF16),
+        pltpu.VMEM((n, span, width), BF16),
         pltpu.VMEM((pairs, groups * stack, LANES), BF16),
         pltpu.VMEM((pairs, groups * stack, LANES), BF16),
         pltpu.VMEM((n, 2 * pairs, span, LANES), BF16),
         pltpu.VMEM((groups, 2 * pairs, span, LANES), BF16),
-        pltpu.VMEM((n, 2 * pairs, span, LANES), BF16),
-        pltpu.VMEM((groups, inner - 1, 2 * pairs, span, LANES), BF16),
-        pltpu.VMEM((groups, 2 * pairs, span, LANES), F32),
         pltpu.VMEM((pairs, 1, groups * stack), F32),
         pltpu.VMEM((pairs, 1, groups * stack), F32),
         pltpu.VMEM((rows, head_width), BF16),
-        pltpu.VMEM((pairs, rows, LANES), F32),
         pltpu.VMEM((rows, width), F32),
         pltpu.VMEM((rows, hidden), BF16),
         pltpu.VMEM((rows, hidden), BF16),
-        pltpu.VMEM((3, rows, width), BF16),
-        pltpu.VMEM((3, rows, width), BF16),
+        pltpu.VMEM((2, groups, 2, span, width), BF16),
+        pltpu.VMEM((2, groups, 2, span, width), BF16),
         pltpu.VMEM((rows, width), F32),
         pltpu.VMEM((pairs, LANES, groups * stack), F32),
+        pltpu.VMEM((n, span // 2, width), BF16),
+        pltpu.VMEM((groups, inner - 1, span // 2, width), BF16),
+        pltpu.VMEM((groups, span, width), BF16),
         pltpu.VMEM((bases[-1], LANES), BF16),
         pltpu.VMEM((bases[-1], LANES), BF16),
         pltpu.VMEM((small_rows, WIDE), F32),
         pltpu.VMEM((bits, small_rows, WIDE), F32),
-        pltpu.VMEM((groups, span, LANES), F32),
-        pltpu.VMEM((groups, span, LANES), F32),
+        pltpu.VMEM((n, LANES), F32),
+        pltpu.VMEM((n, LANES), F32),
+        pltpu.VMEM((span, LANES), F32),
+        pltpu.VMEM((span, LANES), F32),
         pltpu.VMEM((-(-hidden // WIDE // 8) * 8, WIDE), F32),
         pltpu.VMEM((8, width), F32),
         dma((6,)),
+        *[dma((groups,))] * 12,
+        dma((groups, inner)), dma((groups, inner)), dma((groups,)), dma((groups,)), dma((groups,)),
+        dma((4, 2)), dma((4, 2)),
+        dma((groups, inner)), dma((groups, inner)), dma((2,)), dma((2,)),
         *[dma((groups,))] * 8,
-        dma((groups, inner)), dma((groups, inner)),
-        dma((4, 2)), dma((4, 2)),
-        dma((groups, inner)), dma((groups, inner)),
-        *[dma((groups,))] * 8,
-        dma((4, 3, 2 * bits)), dma((4, 3, 2 * bits)), pltpu.SemaphoreType.REGULAR((4, 3, bits)),
+        dma((4, 8, 2 * bits)), dma((4, 8, 2 * bits)), pltpu.SemaphoreType.REGULAR((4, 8, bits)),
         dma((bits,)), dma((bits,)),
         dma((out_copies,)),
     ]
     out_shape = (
-        jax.ShapeDtypeStruct((groups, chunk, width), BF16),
-        jax.ShapeDtypeStruct((groups, chunk, width), BF16),
+        jax.ShapeDtypeStruct((groups, 2, span, width), BF16),
+        jax.ShapeDtypeStruct((groups, 2, span, width), BF16),
         jax.ShapeDtypeStruct((hidden, width), BF16),
         jax.ShapeDtypeStruct((width, hidden), BF16),
         jax.ShapeDtypeStruct((3, width, head_width), BF16),
@@ -811,8 +964,8 @@
             collective_id=0, has_side_effects=True, vmem_limit_bytes=VMEM_BYTES
         ),
     )(
-        layer_input.reshape(groups, chunk, width),
-        cotangent.reshape(groups, chunk, width),
+        layer_input,
+        cotangent,
         w_heads, w_output, w_up, w_down, block_sizes,
         mixing_gain, mixing_shift, feed_gain, feed_shift, bias_up, bias_down,
     )

time: 208 us -> 191 us (0.918)
  Pallas kernels: 207 us -> 190 us
    pallas_call x1, Pallas kernels: 197 us -> 179 us  [local(): pl.pallas_call(functools.partial(fused, (n, groups, span, width, head_wid...]
where the time goes in v3:
time: 191 us
  Pallas kernels  190 us (99%)
    pallas_call x1, Pallas kernels, local(): pl.pallas_call(functools.partial(fused, (n, groups, span, width, head_wid...  179 us
    pallas_call x1, Pallas kernels, local(): pl.pallas_call(functools.partial(widen, len(sources)), grid=(steps,), out...  10.5 us

profile of v3, /device:TPU:0, one launch (start us, length us, event | category | flops | bytes accessed | tf_op | source)
XLA Modules:
  0.0 190.5 jit_solution(8053787479157413542)
XLA Ops:
  0.6 179.3 %shard_map.220 = (bf16[4,2,64,768]{3,2,1,0:T(8,128)(2,1)}, bf16[4,2,64,768]{3,2,1,0:T(8,128)(2,1)}, bf16[1536,768]{1,0:T(8,128)(2,1)}, bf16[768,1536]{1,0:T(8,12...) custom-call(bf16[4,2,64,768]{3,2,1,0:T(8,128)(2,1)} %refs_0_.1, ...), custom_call_target="tpu_custom_call" | custom-call | tf_op jit(solution)/shard_map/pallas_call | solution.py:957
  179.9 10.5 %shard_map.221 = (bf16[512,768]{1,0:T(8,128)(2,1)}, f32[512,768]{1,0:T(8,128)}, f32[3,768,384]{2,1,0:T(8,128)}, f32[384,768]{1,0:T(8,128)}, f32[768,1536]{1,0:T(...) custom-call(bf16[512,768]{1,0:T(8,128)(2,1)} %bitcast.4, ...), custom_call_target="tpu_custom_call" | custom-call | tf_op jit(solution)/shard_map/pallas_call | solution.py:982

commit v4 on v3

--- a/solution.py
+++ b/solution.py
@@ -26,7 +26,7 @@
 PART_ORDERS = ((0, 1, 2, 1, 0, 3), (0, 1, 2, 1, 0, 3), (0, 1, 2), (0, 1, 2))
 TURNS = ((0, (0, 1, 2)), (0, (3, 4, 5)), (1, (0, 1, 2)), (1, (3, 4, 5)), (2, (0, 1, 2)), (3, (0, 1, 2)), (4, (0,)))
 ROUNDS = {
-    "feed_up": 1, "noisy": 1, "g3": 1, "hq": 1, "hk": 1, "plane": 3, "first_back": 2,
+    "half0": 1, "half1": 1, "att_back": 1, "g1p2": 1, "hq": 1, "hk": 1, "plane": 3, "first_back": 2,
 }
 
 
@@ -253,15 +253,34 @@
         noisy_passes[step - 1].start()
     for copy in c_copies:
         copy.start()
+
+    def clean_rows(first):
+        at = pl.ds(first, key_ranks)
+        x = nc[at].reshape(key_ranks * span, width).astype(F32)
+        hat, _ = norm_stats(x)
+        normed = (hat * gain_one[...] + shift_one[...]).astype(BF16)
+        nc[at] = normed.reshape(key_ranks, span, width)
+        table = many(first, key_ranks)
+        for kind in range(2):
+            out = nn(normed, wh[kind + 1])
+            for p in range(pairs):
+                part = out[:, p * LANES:(p + 1) * LANES]
+                low = (part if kind else turn(part, table)).astype(BF16)
+                kv[at, kind * pairs + p] = low.reshape(key_ranks, span, LANES)
+
+    def clean_group(index):
+        plane_pass(index).wait()
+        for block in range(key_blocks):
+            clean_rows(index * inner + block * key_ranks)
+
+    def first_norm(z, carry):
+        hat, _ = norm_stats(xb[z].reshape(chunk, width).astype(F32))
+        n1[z] = (hat * gain_one[...] + shift_one[...]).astype(BF16).reshape(2, span, width)
+        return carry
+
     plane_done(group)
     for copy in clean_passes + noisy_passes:
         copy.wait()
-
-    def first_norm(z, carry):
-        hat, _ = norm_stats(xb[z].reshape(chunk, width).astype(F32))
-        n1[z] = (hat * gain_one[...] + shift_one[...]).astype(BF16).reshape(2, span, width)
-        return carry
-
     lax.fori_loop(0, groups, first_norm, 0)
 
     def queries(z, carry):
@@ -285,19 +304,6 @@
     for step in range(1, groups):
         plane_done(group_peer(groups - step))
 
-    def clean_rows(first):
-        x = nc[first:first + key_ranks].reshape(key_ranks * span, width).astype(F32)
-        hat, _ = norm_stats(x)
-        normed = (hat * gain_one[...] + shift_one[...]).astype(BF16)
-        nc[first:first + key_ranks] = normed.reshape(key_ranks, span, width)
-        table = many(first, key_ranks)
-        for kind in range(2):
-            out = nn(normed, wh[kind + 1])
-            for p in range(pairs):
-                part = out[:, p * LANES:(p + 1) * LANES]
-                low = (part if kind else turn(part, table)).astype(BF16)
-                kv[first:first + key_ranks, kind * pairs + p] = low.reshape(key_ranks, span, LANES)
-
     def clean_mask(index, first_rank, count, shape):
         key = lax.broadcasted_iota(jnp.int32, shape, 0) + first_rank * span
         return key < limit_q + rank * span
@@ -324,9 +330,7 @@
         )
 
     for index in range(groups):
-        plane_pass(index).wait()
-        for block in range(key_blocks):
-            clean_rows(index * inner + block * key_ranks)
+        clean_group(index)
 
         def attend(p, carry, index=index):
             q = qs[p, index * stack:(index + 1) * stack, :]
@@ -394,6 +398,8 @@
         lax.fori_loop(piece * groups // 2, (piece + 1) * groups // 2, second_norm, 0)
 
     small[...] = jnp.zeros_like(small)
+    half_hidden = hidden // 2
+    half_blocks = up_bias_rows // 2
 
     def feed(i, carry):
         cols = pl.ds(pl.multiple_of(i * WIDE, WIDE), WIDE)
@@ -415,7 +421,8 @@
         small[pl.ds(i, 1), :] = sums
         down = tn(hid[:, cols], dy)
         for c in range(col_tiles):
-            at = pl.ds(pl.multiple_of(c * hidden + i * WIDE, WIDE), WIDE)
+            lead = (i // half_blocks) * (col_tiles * half_hidden) + c * half_hidden
+            at = pl.ds(pl.multiple_of(lead + (i % half_blocks) * WIDE, WIDE), WIDE)
             acc[at, :] = down[:, c * LANES:(c + 1) * LANES].astype(BF16)
         return carry
 
@@ -445,10 +452,14 @@
     def partner(bit):
         return peer(me + (1 - 2 * bit_of(bit)) * (1 << bit))
 
-    def sum_steps(job, part):
+    def part_edges(job):
         weights = PART_UNITS[job]
         units = job_rows[job] // n // 16
-        edges = [(2 * sum(weights[:i]) * units + sum(weights)) // (2 * sum(weights)) for i in range(len(weights) + 1)]
+        total = sum(weights)
+        return [(2 * sum(weights[:i]) * units + total) // (2 * total) for i in range(len(weights) + 1)]
+
+    def sum_steps(job, part):
+        edges = part_edges(job)
         base = bases[job] + n * 16 * edges[part]
         s = 16 * (edges[part + 1] - edges[part])
         order = orders[PART_ORDERS[job][part]]
@@ -500,7 +511,11 @@
     outs = [[], [], [], []]
     for c in range(col_tiles):
         at = slice(c * LANES, (c + 1) * LANES)
-        outs[0].append((acc.at[pl.ds(bases[0] + c * hidden, hidden)], down_out.at[:, at]))
+        for part in range(2):
+            lead = bases[0] + (part * col_tiles + c) * (hidden // 2)
+            outs[0].append(
+                (acc.at[pl.ds(lead, hidden // 2)], down_out.at[pl.ds(part * (hidden // 2), hidden // 2), at])
+            )
         outs[2].append((acc.at[pl.ds(bases[2] + c * head_width, head_width)], wout_out.at[:, at]))
     for c in range(hidden // LANES):
         at = slice(c * LANES, (c + 1) * LANES)
@@ -550,12 +565,14 @@
     def begin(job):
         released.add(job)
 
-    lax.fori_loop(0, up_bias_rows, feed, 0)
-    begin(0)
-    take_round()
-    lax.fori_loop(0, up_bias_rows, feed_up, 0)
-    begin(1)
-    point("feed_up")
+    for job, work in enumerate((feed, feed_up)):
+        lax.fori_loop(0, half_blocks, work, 0)
+        if part_edges(job)[3] * 2 == part_edges(job)[-1]:
+            begin(job)
+        point(f"half{job}")
+        lax.fori_loop(half_blocks, up_bias_rows, work, 0)
+        begin(job)
+        point(f"whole{job}")
 
     for piece in range(2):
         lo = piece * half_rows
@@ -620,6 +637,42 @@
 
     lax.fori_loop(0, groups, attended_back, 0)
     point("att_back")
+
+    def feed_out(z, carry):
+        at = chunk_rows(z)
+        fed = (send_h[0, z].astype(F32) + recv_h[0, z].astype(F32)).reshape(chunk, width)
+        dyb[z] = (middle[at, :] + fed + bias_down[...]).astype(BF16).reshape(2, span, width)
+        return carry
+
+    for piece in range(2):
+        head_copy(piece, 2).wait()
+    lax.fori_loop(0, groups, feed_out, 0)
+
+    point("feed_out")
+    def spread(buf, out, ssem, rsem, psend, precv):
+        copies, passes = [], []
+        own = pltpu.make_async_copy(buf.at[group], out.at[group], ssem.at[0])
+        own.start()
+        for step in range(1, groups):
+            to = group_peer(step)
+            source = group_peer(groups - step)
+            copies.append(
+                remote(buf.at[to, :, share], out.at[group, :, share], ssem.at[step], rsem.at[step], peer(to * inner + rank))
+            )
+            passes.append(remote(out.at[source, :, share], out.at[source, :, share], psend.at[step], precv.at[step], sibling))
+        for copy in copies:
+            copy.start()
+        return own, copies, passes
+
+    def pass_on(spread_out):
+        own, copies, passes = spread_out
+        own.wait()
+        for copy, onward in zip(copies, passes):
+            copy.wait()
+            onward.start()
+
+    y_spread = spread(dyb, y_out, y_send, y_recv, yf_send, yf_recv)
+
 
     wout = tn(att[...], n2[...])
     for c in range(col_tiles):
@@ -735,40 +788,6 @@
     core_copy.start()
     point("clean_in")
 
-    def feed_out(z, carry):
-        at = chunk_rows(z)
-        fed = (send_h[0, z].astype(F32) + recv_h[0, z].astype(F32)).reshape(chunk, width)
-        dyb[z] = (middle[at, :] + fed + bias_down[...]).astype(BF16).reshape(2, span, width)
-        return carry
-
-    for piece in range(2):
-        head_copy(piece, 2).wait()
-    lax.fori_loop(0, groups, feed_out, 0)
-
-    point("feed_out")
-    def spread(buf, out, ssem, rsem, psend, precv):
-        copies, passes = [], []
-        own = pltpu.make_async_copy(buf.at[group], out.at[group], ssem.at[0])
-        own.start()
-        for step in range(1, groups):
-            to = group_peer(step)
-            source = group_peer(groups - step)
-            copies.append(
-                remote(buf.at[to, :, share], out.at[group, :, share], ssem.at[step], rsem.at[step], peer(to * inner + rank))
-            )
-            passes.append(remote(out.at[source, :, share], out.at[source, :, share], psend.at[step], precv.at[step], sibling))
-        for copy in copies:
-            copy.start()
-        return own, copies, passes
-
-    def pass_on(spread_out):
-        own, copies, passes = spread_out
-        own.wait()
-        for copy, onward in zip(copies, passes):
-            copy.wait()
-            onward.start()
-
-    y_spread = spread(dyb, y_out, y_send, y_recv, yf_send, yf_recv)
 
     for piece in range(2):
         lo = piece * half_rows
@@ -893,7 +912,7 @@
     bits = int(math.log2(n))
     job_rows, bases = job_layout(n, width, head_width, hidden)
     small_rows = (hidden // WIDE + 5 * (width // WIDE) + 7) // 8 * 8
-    out_copies = width // LANES + hidden // LANES + 3 * pairs + width // LANES
+    out_copies = 2 * (width // LANES) + hidden // LANES + 3 * pairs + width // LANES
     anywhere = pl.BlockSpec(memory_space=pl.ANY)
     vmem = pl.BlockSpec(memory_space=pltpu.VMEM)
     dma = pltpu.SemaphoreType.DMA
@@ -970,7 +989,7 @@
         mixing_gain, mixing_shift, feed_gain, feed_shift, bias_up, bias_down,
     )
     full = (groups, 2, span, width)
-    steps = 8
+    steps = 2
     sources = (y.reshape(rows, width), ig.reshape(rows, width), heads, wout, up, down)
     kinds = (BF16,) + (F32,) * 5
     specs = []

time: 191 us -> 183 us (0.958)
  Pallas kernels: 190 us -> 182 us
    pallas_call x1, Pallas kernels: 179 us -> 173 us  [local(): pl.pallas_call(functools.partial(fused, (n, groups, span, width, head_wid...]
    pallas_call x1, Pallas kernels: 10.5 us -> 8.52 us  [local(): pl.pallas_call(functools.partial(widen, len(sources)), grid=(steps,), out...]
where the time goes in v4:
time: 183 us
  Pallas kernels  182 us (99%)
    pallas_call x1, Pallas kernels, local(): pl.pallas_call(functools.partial(fused, (n, groups, span, width, head_wid...  173 us
    pallas_call x1, Pallas kernels, local(): pl.pallas_call(functools.partial(widen, len(sources)), grid=(steps,), out...  8.52 us

profile of v4, /device:TPU:0, one launch (start us, length us, event | category | flops | bytes accessed | tf_op | source)
XLA Modules:
  0.0 182.7 jit_solution(6563977609793092706)
XLA Ops:
  0.6 173.4 %shard_map.220 = (bf16[4,2,64,768]{3,2,1,0:T(8,128)(2,1)}, bf16[4,2,64,768]{3,2,1,0:T(8,128)(2,1)}, bf16[1536,768]{1,0:T(8,128)(2,1)}, bf16[768,1536]{1,0:T(8,12...) custom-call(bf16[4,2,64,768]{3,2,1,0:T(8,128)(2,1)} %refs_0_.1, ...), custom_call_target="tpu_custom_call" | custom-call | tf_op jit(solution)/shard_map/pallas_call | solution.py:976
  174.0 8.5 %shard_map.221 = (bf16[512,768]{1,0:T(8,128)(2,1)}, f32[512,768]{1,0:T(8,128)}, f32[3,768,384]{2,1,0:T(8,128)}, f32[384,768]{1,0:T(8,128)}, f32[768,1536]{1,0:T(...) custom-call(bf16[512,768]{1,0:T(8,128)(2,1)} %bitcast.4, ...), custom_call_target="tpu_custom_call" | custom-call | tf_op jit(solution)/shard_map/pallas_call | solution.py:1001

commit v5 on v4

--- a/solution.py
+++ b/solution.py
@@ -22,7 +22,7 @@
 VMEM_BYTES = 66_900_000
 
 
-PART_UNITS = ((7, 7, 4, 7, 7, 4), (7, 7, 4, 7, 7, 4), (7, 7, 4), (7, 7, 4))
+PART_UNITS = ((6, 6, 6, 8, 7, 3), (7, 8, 3, 8, 7, 3), (7, 8, 3), (7, 7, 4))
 PART_ORDERS = ((0, 1, 2, 1, 0, 3), (0, 1, 2, 1, 0, 3), (0, 1, 2), (0, 1, 2))
 TURNS = ((0, (0, 1, 2)), (0, (3, 4, 5)), (1, (0, 1, 2)), (1, (3, 4, 5)), (2, (0, 1, 2)), (3, (0, 1, 2)), (4, (0,)))
 ROUNDS = {

time: 183 us -> 180 us (0.984)
  Pallas kernels: 182 us -> 179 us
    pallas_call x1, Pallas kernels: 173 us -> 171 us  [local(): pl.pallas_call(functools.partial(fused, (n, groups, span, width, head_wid...]
where the time goes in v5:
time: 180 us
  Pallas kernels  179 us (99%)
    pallas_call x1, Pallas kernels, local(): pl.pallas_call(functools.partial(fused, (n, groups, span, width, head_wid...  171 us
    pallas_call x1, Pallas kernels, local(): pl.pallas_call(functools.partial(widen, len(sources)), grid=(steps,), out...  8.52 us

profile of v5, /device:TPU:0, one launch (start us, length us, event | category | flops | bytes accessed | tf_op | source)
XLA Modules:
  0.0 180.0 jit_solution(8090718271216011283)
XLA Ops:
  0.6 170.7 %shard_map.220 = (bf16[4,2,64,768]{3,2,1,0:T(8,128)(2,1)}, bf16[4,2,64,768]{3,2,1,0:T(8,128)(2,1)}, bf16[1536,768]{1,0:T(8,128)(2,1)}, bf16[768,1536]{1,0:T(8,12...) custom-call(bf16[4,2,64,768]{3,2,1,0:T(8,128)(2,1)} %refs_0_.1, ...), custom_call_target="tpu_custom_call" | custom-call | tf_op jit(solution)/shard_map/pallas_call | solution.py:976
  171.3 8.5 %shard_map.221 = (bf16[512,768]{1,0:T(8,128)(2,1)}, f32[512,768]{1,0:T(8,128)}, f32[3,768,384]{2,1,0:T(8,128)}, f32[384,768]{1,0:T(8,128)}, f32[768,1536]{1,0:T(...) custom-call(bf16[512,768]{1,0:T(8,128)(2,1)} %bitcast.4, ...), custom_call_target="tpu_custom_call" | custom-call | tf_op jit(solution)/shard_map/pallas_call | solution.py:1001
